TPU v7x, 256 devices: a whole 4x4x8 slice. The times are simulated.
256 devices in a mesh: ctx: 32 (over z, y), head: 8 (over x, core).
Axes of the slice: x: 4, y: 4, z: 8, core: 2. Of those that a mesh axis runs over, the one named last changes fastest.
Arguments:
- queries: bfloat16 [16384, 4096], P('ctx', 'head'), may hold values from -6 to 6
- keys: bfloat16 [16384, 8192], P('ctx', 'head'), may hold values from -6 to 6
- values: bfloat16 [16384, 8192], P('ctx', 'head'), may hold values from -6 to 6
- betas: float32 [16384, 64], P('ctx', 'head'), may hold values from 0 to 2
- initial_state: float32 [32, 128, 128], P('head'), may hold values from -48 to 48
- out_gain: float32 [4096], P('head'), may hold values from 0.1 to 1.9
Outputs:
- mixed: bfloat16 [16384, 4096], P(('ctx', 'head'))
All inputs are finite; a program needn't handle non-finite values.
Results may differ from a plain program's by a relative error of at most 0.0033.
Values may be sent and summed in bfloat16 or wider, within the bound.
No kernel may reach another device: no remote copies, remote signals or barrier semaphores. Data moves between devices by JAX's collectives and lax.ppermute only.
A program may use at most 128 MiB of HBM per device.

v0:
```python
import jax
import jax.numpy as jnp
from jax import lax
from jax.sharding import PartitionSpec as P

DK = 128
DV = 128
GROUP = 64


HIGH = lax.Precision.HIGHEST


def carried_in(part, axis, combine, identity):
    place = lax.axis_index(axis)
    gathered = jax.tree.map(lambda a: lax.all_gather(a, axis), part)
    state = jax.tree.map(lambda a, e: jnp.zeros_like(a) + jnp.asarray(e, a.dtype), part, identity)

    def one(turn, state):
        return combine(
            state, jax.tree.map(lambda a: lax.dynamic_index_in_dim(a, turn, 0, False), gathered)
        )

    return lax.fori_loop(0, place, one, state)


def normalize(x):
    return x * lax.rsqrt(jnp.sum(x * x, -1, keepdims=True) + 1e-06)


def prepare(queries, keys, values, betas, heads):
    blocks = queries.shape[0] // GROUP
    qf = normalize(queries.astype(jnp.float32).reshape(blocks, GROUP, heads, DK))
    kf = normalize(keys.astype(jnp.float32).reshape(blocks, GROUP, heads, 2, DK))
    vf = values.astype(jnp.float32).reshape(blocks, GROUP, heads, 2, DV)
    bf = betas.reshape(blocks, GROUP, heads, 2)
    qc = qf.transpose(0, 2, 1, 3)
    kc = kf.transpose(0, 2, 1, 3, 4).reshape(blocks, heads, 2 * GROUP, DK)
    vc = vf.transpose(0, 2, 1, 3, 4).reshape(blocks, heads, 2 * GROUP, DV)
    bc = bf.transpose(0, 2, 1, 3).reshape(blocks, heads, 2 * GROUP)
    return (qc, kc, vc, bc)


def wy_factors(kc, vc, bc):
    items = kc.shape[-2]
    gram = jnp.einsum("...ik,...jk->...ij", kc, kc, precision=HIGH)
    system = jnp.tril(gram * bc[..., :, None], -1) + jnp.eye(items, dtype=jnp.float32)
    rhs = bc[..., :, None] * jnp.concatenate([kc, vc], -1)
    sol = lax.linalg.triangular_solve(system, rhs, left_side=True, lower=True, unit_diagonal=True)
    return (sol[..., :DK], sol[..., DK:])


def visible_mask():
    item_pos = jnp.arange(2 * GROUP, dtype=jnp.int32)[None, :]
    query_pos = jnp.arange(GROUP, dtype=jnp.int32)[:, None]
    return (item_pos <= 2 * query_pos + 1).astype(jnp.float32)


def apply_map(state, transition, added):
    return jnp.einsum("hvk,hkm->hvm", state, transition, precision=HIGH) + added


def combine_maps(early, late):
    merged_outcome = jnp.einsum("hab,hbc->hac", early[0], late[0], precision=HIGH)
    return (merged_outcome, apply_map(early[1], late[0], late[1]))


def body(queries, keys, values, betas, initial_state, out_gain):
    rows = queries.shape[0]
    heads = queries.shape[1] // DK
    qc, kc, vc, bc = prepare(queries, keys, values, betas, heads)
    wmat, umat = wy_factors(kc, vc, bc)
    scores = jnp.einsum("nhck,nhik->nhci", qc, kc, precision=HIGH) * visible_mask()
    eye_maps = jnp.broadcast_to(jnp.eye(DK, dtype=jnp.float32), (heads, DK, DK))
    zero_state = jnp.zeros((heads, DV, DK), jnp.float32)

    def compose(carry, inputs):
        wblock, kblock, ublock = inputs
        passage_result = jnp.einsum("hrk,hik->hri", carry, wblock, precision=HIGH)
        carry = carry - jnp.einsum("hri,hik->hrk", passage_result, kblock, precision=HIGH)
        written = jnp.einsum("hiv,hik->hvk", ublock, kblock, precision=HIGH)
        carry = carry + jnp.concatenate([jnp.zeros((heads, DK, DK), jnp.float32), written], 1)
        return (carry, None)

    start_maps = jnp.concatenate([eye_maps, zero_state], 1)
    whole, unused = lax.scan(compose, start_maps, (wmat, kc, umat))
    transition = whole[:, :DK]
    added = whole[:, DK:]
    before = carried_in((transition, added), "ctx", combine_maps, (eye_maps, zero_state))
    entry = apply_map(initial_state, before[0], before[1])

    def advance(state, inputs):
        qblock, kblock, wblock, ublock, sblock = inputs
        fresh = ublock - jnp.einsum("hik,hvk->hiv", wblock, state, precision=HIGH)
        result = jnp.einsum("hck,hvk->hcv", qblock, state, precision=HIGH)
        result = result + jnp.einsum("hci,hiv->hcv", sblock, fresh, precision=HIGH)
        state = state + jnp.einsum("hiv,hik->hvk", fresh, kblock, precision=HIGH)
        return (state, result)

    final_state, outs = lax.scan(advance, entry, (qc, kc, wmat, umat, scores))
    scale = lax.rsqrt(jnp.mean(outs * outs, -1, keepdims=True) + 1e-06)
    normed = outs * scale * out_gain.reshape(1, heads, 1, DV)
    local_out = normed.transpose(0, 2, 1, 3).reshape(rows, heads * DV).astype(jnp.bfloat16)
    return lax.all_to_all(local_out, "head", split_axis=0, concat_axis=1, tiled=True)


def solution(mesh):
    placed = (
        P("ctx", "head"),
        P("ctx", "head"),
        P("ctx", "head"),
        P("ctx", "head"),
        P("head", None, None),
        P("head"),
    )
    return jax.shard_map(
        body, mesh=mesh, in_specs=placed, out_specs=P(("ctx", "head"), None), check_vma=False
    )
```

profile of v0, /device:TPU:248, one launch (start us, length us, event | category | flops | bytes accessed | tf_op | source)
XLA Modules:
  0.0 784.2 jit_solution(11596532230022436802)
XLA Ops:
  6.6 3.2 reshape.109
  9.8 3.2 multiply_reduce_fusion
  13.2 2.5 multiply_bitcast_fusion
  17.2 5.8 add_bitcast_fusion
  23.0 315.8 %custom-call.3 = f32[8,4,1,128,128]{3,4,2,1,0:T(8,128)} custom-call(f32[8,4,1,128,128]{4,3,2,1,0:T(8,128)} %add_bitcast_fusion), custom_call_target="InvertDiagBlocksLowerTriangular" | custom-call | tf_op jit(solution)/shard_map/triangular_solve | solution.py:49
  338.9 4.1 reshape.116
  343.0 2.8 copy.67
  345.8 4.8 fusion.36
  350.6 2.5 fusion.48
  353.2 30.4 %while.34 = (s32[]{:T(128)}, f32[4,256,128]{2,1,0:T(8,128)S(1)}, f32[8,4,128,128]{3,2,1,0:T(8,128)}, f32[8,4,128,128]{3,2,1,0:T(8,128)S(1)}, f32[8,4,128,128]{3,2,1,0:T(8,128)}, /*index=5*/s32[]{:T(128)}) while((s32[]{:T(128)}, f32[4,256,128]{2,1,0:T(8,128)S(1)}, f32[8,4,128,128]{3,2,1,0:T(8,128)}, f32[8,4,128,128]{3,2,1,0:T(8,128)S(1)}, ...), condition=%wide.region_2.3_spmd, body=%wide.region_1.0_spmd.sunk | while | flops 503578624 | bytes 4195913 | solution.py:86
  389.2 5.1 convolution_multiply_fusion
  394.4 85.1 %all-gather.5.cloned.1.call-done = f32[128,128,128]{2,1,0:T(8,128)} async-done(((f32[4,128,128]{2,1,0:T(8,128)}), f32[128,128,128]{2,1,0:T(8,128)}) %all-gather.5.cloned.1.call-update) | async-done | bytes 8388624 | tf_op jit(solution)/shard_map/all_gather | solution.py:16
  479.5 98.2 %all-gather.7.cloned.1.call-done = f32[128,128,128]{2,1,0:T(8,128)} async-done(((f32[4,128,128]{2,1,0:T(8,128)}), f32[128,128,128]{2,1,0:T(8,128)}) %all-gather.7.cloned.1.call-update) | async-done | bytes 8388624 | tf_op jit(solution)/shard_map/all_gather | solution.py:16
  577.8 134.0 %while.35 = (s32[]{:T(128)}, f32[4,128,128]{1,2,0:T(8,128)S(1)}, f32[4,128,128]{1,2,0:T(8,128)S(1)}, s32[]{:T(128)}, f32[32,4,128,128]{3,2,1,0:T(8,128)}, /*inde...) while((s32[]{:T(128)}, f32[4,128,128]{1,2,0:T(8,128)S(1)}, f32[4,128,128]{1,2,0:T(8,128)S(1)}, ...), condition=%wide.region_4.5_spmd, body=%wide.region_3.4_spmd.sunk | while | flops 201392128 | bytes 3932299 | solution.py:24
  579.0 1.6 fusion.101
  583.3 1.6 fusion.101
  587.6 1.6 fusion.101
  591.9 1.6 fusion.101
  596.3 1.6 fusion.101
  600.6 1.6 fusion.101
  604.9 1.6 fusion.101
  609.2 1.6 fusion.101
  613.5 1.6 fusion.101
  617.9 1.6 fusion.101
  622.2 1.6 fusion.101
  626.5 1.6 fusion.101
  630.8 1.6 fusion.101
  635.2 1.6 fusion.101
  639.5 1.6 fusion.101
  643.8 1.6 fusion.101
  648.1 1.6 fusion.101
  652.4 1.6 fusion.101
  656.8 1.6 fusion.101
  661.1 1.6 fusion.101
  665.4 1.6 fusion.101
  669.7 1.6 fusion.101
  674.0 1.6 fusion.101
  678.4 1.6 fusion.101
  682.7 1.6 fusion.101
  687.0 1.6 fusion.101
  695.6 1.6 fusion.101
  700.0 1.6 fusion.101
  704.3 1.6 fusion.101
  708.6 1.6 fusion.101
  712.6 46.3 %while.36 = (s32[]{:T(128)}, f32[4,128,128]{2,1,0:T(8,128)S(1)}, f32[8,4,64,128]{3,2,1,0:T(8,128)}, f32[8,4,128,128]{3,2,1,0:T(8,128)}, f32[8,4,128,128]{3,2,1,0...) while((s32[]{:T(128)}, f32[4,128,128]{2,1,0:T(8,128)S(1)}, ...), condition=%wide.region_7.8_spmd, body=%wide.region_6.7_spmd.sunk | while | flops 302153728 | bytes 3279457 | solution.py:100
  712.6 1.7 convolution_subtract_fusion.3
  715.8 1.9 fusion.111
  718.4 1.7 convolution_subtract_fusion.3
  721.6 1.9 fusion.111
  724.2 1.7 convolution_subtract_fusion.3
  727.4 1.9 fusion.111
  730.0 1.7 convolution_subtract_fusion.3
  733.2 1.9 fusion.111
  735.8 1.7 convolution_subtract_fusion.3
  739.0 1.9 fusion.111
  741.6 1.7 convolution_subtract_fusion.3
  744.8 1.9 fusion.111
  747.3 1.7 convolution_subtract_fusion.3
  750.6 1.9 fusion.111
  753.1 1.7 convolution_subtract_fusion.3
  756.3 1.9 fusion.111
  758.9 1.6 multiply_reduce_fusion.1
  760.5 1.6 copy_bitcast_fusion
  762.1 14.4 %all_to_all.16 = bf16[8,64,512]{2,1,0:T(8,128)(2,1)S(1)} all-to-all(bf16[8,64,512]{2,1,0:T(8,128)(2,1)S(1)} %copy_bitcast_fusion), channel_id=1, replica_groups=mesh['ctx'=32,'head'=8] {'head'}, dimensions={0} | all-to-all | bytes 1048576 | tf_op jit(solution)/shard_map/all_to_all | solution.py:104
  (234 shorter events, 141.3 us)
Async XLA Ops:
  6.5 705.3 %copy-start = (f32[4,128,128]{2,1,0:T(8,128)S(1)}, f32[4,128,128]{2,1,0:T(8,128)}, u32[]{:S(2)}) copy-start(f32[4,128,128]{2,1,0:T(8,128)} %param.16) | copy-start | bytes 786436
  6.5 473.0 %all-gather.5.cloned.1.call-start = ((), (), s32[]{:S(2)}) async-start(), calls=%async_computation.1 | async-start | bytes 8650752 | tf_op jit(solution)/shard_map/all_gather | solution.py:16
  15.7 1.2 copy-start.2
  343.0 2.8 copy-start.1
  384.5 193.3 %all-gather.7.cloned.1.call-start = ((), (), s32[]{:S(2)}) async-start(), calls=%async_computation.2 | async-start | bytes 8650752 | tf_op jit(solution)/shard_map/all_gather | solution.py:16
  712.6 47.9 %copy-start.3 = (f32[512]{0:T(512)S(1)}, f32[512]{0:T(512)}, u32[]{:S(2)}) copy-start(f32[512]{0:T(512)} %param.17) | copy-start | bytes 6148
Sparse Core Ops, SparseCore 0:
  384.6 94.8 all-gather.4
  482.1 95.6 all-gather.6
where the time goes:
time: 788 us; the launch traced here: 784 us
  other arithmetic  326 us (41%)
  matrix products  189 us (24%)
  waiting for transfers between devices  184 us (23%)
  local copies, waits for them, and re-layouts  53.8 us (7%)
  blocking collectives  14.4 us (2%)
  between operations  13.6 us (2%)
    another operation x4, other arithmetic, wy_factors(): lax.linalg.triangular_solve(system, rhs, left_side=True, lower=True, unit...  316 us
    all_gather x2, waiting for transfers between devices, carried_in(): gathered = jax.tree.map(lambda a: lax.all_gather(a, axis), part)  183 us
    dot_general x32, matrix products, apply_map(): return jnp.einsum('hvk,hkm->hvm', state, transition, precision=HIGH) + added  49 us
    dot_general x31, matrix products, combine_maps(): jnp.einsum('hab,hbc->hac', early[0], late[0], precision=HIGH)  48.2 us
    dynamic_slice x62, local copies, waits for them, and re-layouts, one(): lax.dynamic_index_in_dim(a, turn, 0, False)  34.1 us
  transfers between devices with their start and end apart: 2, of which 2 were waited for; matrix products, arithmetic and copies ran while one was open for 1% of the time, Pallas kernels for 0%

commit v1 on v0

v1 whole, which is shorter than its diff:
```python
import functools
import jax
import jax.numpy as jnp
from jax import lax
from jax.experimental import pallas as pl
from jax.experimental.pallas import tpu as pltpu
from jax.sharding import PartitionSpec as P

D = 128
HALF = 64
ITEMS = 128
BLOCKS = 8
HEADS = 4
NY = 4
NZ = 8
F32 = jnp.float32
BF16 = jnp.bfloat16
VMEM_LIMIT = 48 * 1024 * 1024


def split(x):
    hi = x.astype(BF16)
    lo = (x - hi.astype(F32)).astype(BF16)
    return hi, lo


def mm(a, b):
    return lax.dot_general(a, b, (((1,), (0,)), ((), ())), preferred_element_type=F32)


def mm_nt(a, b):
    return lax.dot_general(a, b, (((1,), (1,)), ((), ())), preferred_element_type=F32)


def mm_tn(a, b):
    return lax.dot_general(a, b, (((0,), (0,)), ((), ())), preferred_element_type=F32)


def both(parts, axis):
    return jnp.concatenate(parts, axis)


def narrow3(ah, al, bh, bl):
    right = both([bh, bl], 1)
    out = mm(both([ah, al], 1), both([right, right], 0))
    return out[:, :D] + out[:, D:]


def wide3(ah, al, bh, bl):
    return mm(both([ah, al], 1), both([bh, bh], 0)) + mm(ah, bl)


def join(early, late):
    out = wide3(*split(late[:, :D]), *split(early))
    return both([out[:, :D], out[:, D:] + late[:, D:]], 1)


def order(shape, axis):
    place = lax.broadcasted_iota(jnp.int32, shape, axis)
    return 2 * (place % HALF) + place // HALF


def block_keys(ref, b):
    rows = slice(b * HALF, (b + 1) * HALF)
    return both([ref[rows, :D], ref[rows, D:]], 0)


def local_maps_kernel(k_ref, v_ref, b_ref, wu_ref, r_ref, tot_ref):
    shape = (ITEMS, ITEMS)
    ni, nj = order(shape, 0), order(shape, 1)
    eye = (ni == nj).astype(F32)
    masks = []
    for level in range(7):
        hit = ((ni >> (level + 1)) == (nj >> (level + 1))) & ((ni >> level) > (nj >> level))
        masks.append(hit.astype(F32))
    low = [m.astype(BF16) for m in masks]
    ks = [block_keys(k_ref, b) for b in range(BLOCKS)]
    grams = [mm_nt(k, k) for k in ks]
    squares = both([jnp.sum(g * eye, 0, keepdims=True) for g in grams], 0)
    rk = lax.rsqrt(squares + 1e-06)
    beta_rk = b_ref[0] * rk
    beta_rk2 = beta_rk * rk
    columns = beta_rk2.T
    lows = [columns[:, b : b + 1] * g for b, g in enumerate(grams)]
    inv = [eye - l * masks[0] for l in lows]
    pieces = [split(l) for l in lows]
    for level in range(1, 7):
        m = low[level]
        cut = [split(t) for t in inv]
        step = [narrow3(*t, p[0] * m, p[1] * m) for t, p in zip(cut, pieces)]
        inv = [t - narrow3(*split(x), *c) for t, x, c in zip(inv, step, cut)]
    maps = []
    for b in range(BLOCKS):
        v = block_keys(v_ref, b)
        w = mm(both(split(inv[b] * beta_rk2[b : b + 1]), 1), both([ks[b], ks[b]], 0))
        u = mm(both(split(inv[b] * beta_rk[b : b + 1]), 1), both([v, v], 0))
        wh, wl = split(w)
        uh, ul = split(u)
        wu = both([wh, uh, wl, ul], 1)
        wu_ref[0, b] = wu
        r = mm_tn(ks[b], wu)
        r = r[:, : 2 * D] + r[:, 2 * D :]
        maps.append(both([eye_minus(r[:, :D]), r[:, D:]], 1))
    total = maps[0]
    r_ref[0, 0] = jnp.zeros((D, 4 * D), BF16)
    for b in range(1, BLOCKS):
        th, tl = split(total)
        r_ref[0, b] = both([th, tl], 1)
        out = wide3(*split(maps[b][:, :D]), th, tl)
        total = both([out[:, :D], out[:, D:] + maps[b][:, D:]], 1)
    tot_ref[0] = total


def eye_minus(x):
    i = lax.broadcasted_iota(jnp.int32, x.shape, 0)
    j = lax.broadcasted_iota(jnp.int32, x.shape, 1)
    return (i == j).astype(F32) - x


def local_maps(keys, values, betas):
    return pl.pallas_call(
        local_maps_kernel,
        grid=(HEADS,),
        in_specs=[
            pl.BlockSpec((BLOCKS * HALF, 2 * D), lambda h: (0, h)),
            pl.BlockSpec((BLOCKS * HALF, 2 * D), lambda h: (0, h)),
            pl.BlockSpec((1, BLOCKS, ITEMS), lambda h: (h, 0, 0)),
        ],
        out_specs=[
            pl.BlockSpec((1, BLOCKS, ITEMS, 4 * D), lambda h: (h, 0, 0, 0)),
            pl.BlockSpec((1, BLOCKS, D, 4 * D), lambda h: (h, 0, 0, 0)),
            pl.BlockSpec((1, D, 2 * D), lambda h: (h, 0, 0)),
        ],
        out_shape=[
            jax.ShapeDtypeStruct((HEADS, BLOCKS, ITEMS, 4 * D), BF16),
            jax.ShapeDtypeStruct((HEADS, BLOCKS, D, 4 * D), BF16),
            jax.ShapeDtypeStruct((HEADS, D, 2 * D), F32),
        ],
        compiler_params=pltpu.CompilerParams(vmem_limit_bytes=VMEM_LIMIT),
        name="local_maps",
    )(keys, values, betas)


def outputs_kernel(q_ref, k_ref, wu_ref, r_ref, qe_ref, ol_ref):
    shape = (HALF, ITEMS)
    seen = (
        lax.broadcasted_iota(jnp.int32, shape, 1) % HALF <= lax.broadcasted_iota(jnp.int32, shape, 0)
    ).astype(F32)
    for b in range(BLOCKS):
        rows = slice(b * HALF, (b + 1) * HALF)
        q = q_ref[rows, :]
        qf = q.astype(F32)
        sh, sl = split(mm_nt(q, block_keys(k_ref, b)) * seen)
        wu = wu_ref[0, b]
        x = wide3(sh, sl, wu[:, : 2 * D], wu[:, 2 * D :])
        qe, ol = qf - x[:, :D], x[:, D:]
        if b:
            r = r_ref[0, b]
            e = wide3(*split(qe), r[:, : 2 * D], r[:, 2 * D :])
            qe, ol = e[:, :D], e[:, D:] + ol
        rq = lax.rsqrt(jnp.sum(qf * qf, -1, keepdims=True) + 1e-06)
        qe_ref[0, rows, :] = qe * rq
        ol_ref[0, rows, :] = ol * rq


def local_outputs(queries, keys, wu, prefixes):
    flops = 2 * HEADS * BLOCKS * HALF * D * D * 16
    return pl.pallas_call(
        outputs_kernel,
        grid=(HEADS,),
        in_specs=[
            pl.BlockSpec((BLOCKS * HALF, D), lambda h: (0, h)),
            pl.BlockSpec((BLOCKS * HALF, 2 * D), lambda h: (0, h)),
            pl.BlockSpec((1, BLOCKS, ITEMS, 4 * D), lambda h: (h, 0, 0, 0)),
            pl.BlockSpec((1, BLOCKS, D, 4 * D), lambda h: (h, 0, 0, 0)),
        ],
        out_specs=[
            pl.BlockSpec((1, BLOCKS * HALF, D), lambda h: (h, 0, 0)),
            pl.BlockSpec((1, BLOCKS * HALF, D), lambda h: (h, 0, 0)),
        ],
        out_shape=[jax.ShapeDtypeStruct((HEADS, BLOCKS * HALF, D), F32)] * 2,
        compiler_params=pltpu.CompilerParams(vmem_limit_bytes=VMEM_LIMIT),
        cost_estimate=pl.CostEstimate(flops=flops, bytes_accessed=12 * 1024 * 1024, transcendentals=0),
        name="local_outputs",
    )(queries, keys, wu, prefixes)


def in_vmem(n):
    return [pl.BlockSpec(memory_space=pltpu.VMEM)] * n


def in_smem():
    return [pl.BlockSpec(memory_space=pltpu.SMEM)]


def row_maps_kernel(me_ref, own_ref, r1, r2, r3, pre_ref, tot_ref, held):
    y = me_ref[0]
    held[y] = own_ref[y]
    for s, ref in ((1, r1), (2, r2), (3, r3)):
        held[(y + NY - s) % NY] = ref[...]
    total = held[0]
    for i in range(1, NY):
        pre_ref[i - 1] = total
        total = join(total, held[i])
    tot_ref[...] = total


def plane_maps_kernel(me_ref, own_ref, r1, r2, r3, s0_ref, pre_ref, end_ref, s0t_ref, held):
    y, z = me_ref[0], me_ref[1] % 4
    held[z] = own_ref[...]
    for s, ref in ((1, r1), (2, r2), (3, r3)):
        held[(z + 4 - s) % 4] = ref[...]
    start = s0_ref[y].T
    s0t_ref[...] = start
    total = held[0]
    pre_ref[...] = total
    for i in range(1, 4):
        @pl.when(z == i)
        def _():
            pre_ref[...] = total
        total = join(total, held[i])
    end_ref[...] = apply(total, start)


def apply(m, state):
    return narrow3(*split(m[:, :D]), *split(state)) + m[:, D:]


def states_kernel(me_ref, s0t_ref, mid_ref, pre_ref, rows_ref, out_ref):
    z = me_ref[1]
    late = (z >= 4).astype(F32)
    base = s0t_ref[...] * (1.0 - late) + mid_ref[...] * late
    inner = ((z % 4) > 0).astype(F32)
    moved = apply(pre_ref[...], base)
    state = moved * inner + base * (1.0 - inner)
    out_ref[0] = state
    for i in range(1, NY):
        out_ref[i] = apply(rows_ref[i - 1], state)


def finish_kernel(me_ref, s_own, s1, s2, s3, qe_ref, ol_ref, g_ref, out_ref):
    y = me_ref[0]
    for s in range(NY):
        h = (y + NY - s) % NY
        state = s_own[y] if s == 0 else (s1, s2, s3)[s - 1][...]
        raw = narrow3(*split(qe_ref[h]), *split(state)) + ol_ref[h]
        scale = lax.rsqrt(jnp.mean(raw * raw, -1, keepdims=True) + 1e-06)
        out_ref[:, pl.ds(pl.multiple_of(h * D, D), D)] = (raw * scale * g_ref[h]).astype(BF16)


def call(kernel, n_in, out_shape, scratch=(), name=None):
    return pl.pallas_call(
        kernel,
        in_specs=in_smem() + in_vmem(n_in),
        out_specs=jax.tree.map(lambda _: pl.BlockSpec(memory_space=pltpu.VMEM), out_shape),
        out_shape=out_shape,
        scratch_shapes=list(scratch),
        compiler_params=pltpu.CompilerParams(vmem_limit_bytes=VMEM_LIMIT),
        name=name,
    )


def shift_y(s):
    return [(z * NY + y, z * NY + (y + s) % NY) for z in range(NZ) for y in range(NY)]


def shift_z(s):
    return [
        (z * NY + y, (z // 4 * 4 + (z % 4 + s) % 4) * NY + y) for z in range(NZ) for y in range(NY)
    ]


ACROSS = [(z * NY + y, (z + 4) * NY + y) for z in range(4) for y in range(NY)]


def body(queries, keys, values, betas, initial_state, out_gain):
    f32 = lambda *shape: jax.ShapeDtypeStruct(shape, F32)
    place = lax.axis_index("ctx").astype(jnp.int32)
    y, z = place % NY, place // NY
    me = jnp.stack([y, z])
    bt = betas.reshape(BLOCKS, HALF, HEADS, 2).transpose(2, 0, 3, 1).reshape(HEADS, BLOCKS, ITEMS)
    wu, prefixes, total = local_maps(keys, values, bt)

    def exchange(array):
        return [
            lax.ppermute(lax.dynamic_index_in_dim(array, (y + s) % NY, 0, False), "ctx", shift_y(s))
            for s in (1, 2, 3)
        ]

    rows_pre, row_total = call(
        row_maps_kernel, 4, [f32(3, D, 2 * D), f32(D, 2 * D)], [pltpu.VMEM((4, D, 2 * D), F32)], "row_maps"
    )(me, total, *exchange(total))
    others = [lax.ppermute(row_total, "ctx", shift_z(s)) for s in (1, 2, 3)]
    plane_pre, end, start = call(
        plane_maps_kernel,
        5,
        [f32(D, 2 * D), f32(D, D), f32(D, D)],
        [pltpu.VMEM((4, D, 2 * D), F32)],
        "plane_maps",
    )(me, row_total, *others, initial_state)
    mid = lax.ppermute(end, "ctx", ACROSS)
    states = call(states_kernel, 4, f32(NY, D, D), (), "states")(me, start, mid, plane_pre, rows_pre)
    qe, ol = local_outputs(queries, keys, wu, prefixes)
    local_out = call(
        finish_kernel, 7, jax.ShapeDtypeStruct((BLOCKS * HALF, HEADS * D), BF16), (), "finish"
    )(me, states, *exchange(states), qe, ol, out_gain.reshape(HEADS, 1, D))
    return lax.all_to_all(local_out, "head", split_axis=0, concat_axis=1, tiled=True)


def solution(mesh):
    placed = (
        P("ctx", "head"),
        P("ctx", "head"),
        P("ctx", "head"),
        P("ctx", "head"),
        P("head", None, None),
        P("head"),
    )
    return jax.shard_map(
        body, mesh=mesh, in_specs=placed, out_specs=P(("ctx", "head"), None), check_vma=False
    )
```

time: 788 us -> 90.4 us (0.11)
  the two profiles are of different devices: /device:TPU:248 before, /device:TPU:32 now
where the time goes in v1:
time: 90.4 us; the launch traced here: 89.9 us
  Pallas kernels  31.4 us (35%)
  starting transfers between devices  23.9 us (26%)
  waiting for transfers between devices  15.5 us (17%)
  blocking collectives  14.6 us (16%)
  local copies, waits for them, and re-layouts  4.29 us (5%)
    pallas_call x1, Pallas kernels, local_maps(): pl.pallas_call(local_maps_kernel, grid=(HEADS,), in_specs=[pl.BlockSpec((...  17.9 us
    all_to_all x1, blocking collectives, body(): lax.all_to_all(local_out, 'head', split_axis=0, concat_axis=1, tiled=True)  14.6 us
    ppermute x6, starting transfers between devices, exchange(): lax.ppermute(lax.dynamic_index_in_dim(array, (y + s) % NY, 0, False), 'ct...  10.6 us
    ppermute x3, waiting for transfers between devices, body(): others = [lax.ppermute(row_total, 'ctx', shift_z(s)) for s in (1, 2, 3)]  9.01 us
    pallas_call x1, Pallas kernels, local_outputs(): pl.pallas_call(outputs_kernel, grid=(HEADS,), in_specs=[pl.BlockSpec((BLO...  8.89 us
    ppermute x1, starting transfers between devices, body(): mid = lax.ppermute(end, 'ctx', ACROSS)  7.91 us
    ppermute x3, starting transfers between devices, body(): others = [lax.ppermute(row_total, 'ctx', shift_z(s)) for s in (1, 2, 3)]  5.37 us
    ppermute x6, waiting for transfers between devices, exchange(): lax.ppermute(lax.dynamic_index_in_dim(array, (y + s) % NY, 0, False), 'ct...  4.63 us
  transfers between devices with their start and end apart: 10, of which 6 were waited for; matrix products, arithmetic and copies ran while one was open for 0% of the time, Pallas kernels for 10%

profile of v1, /device:TPU:32, one launch (start us, length us, event | category | flops | bytes accessed | tf_op | source)
XLA Modules:
  0.0 89.9 jit_solution(5539803244634165357)
XLA Ops:
  0.0 0.0 copy-start.4
  0.0 0.8 reshape.12
  0.9 0.1 reshape.13.b_ref
  0.9 0.0 copy-start
  0.9 1.2 %copy-done = bf16[512,1024]{1,0:T(8,128)(2,1)S(1)} copy-done((bf16[512,1024]{1,0:T(8,128)(2,1)S(1)}, bf16[512,1024]{1,0:T(8,128)(2,1)}, u32[]{:S(2)}) %copy-start) | copy-done | bytes 1048600
  2.2 0.0 copy-start.2
  2.2 1.2 %copy-done.2 = bf16[512,1024]{1,0:T(8,128)(2,1)S(1)} copy-done((bf16[512,1024]{1,0:T(8,128)(2,1)S(1)}, bf16[512,1024]{1,0:T(8,128)(2,1)}, u32[]{:S(2)}) %copy-start.2) | copy-done | bytes 1048600
  3.4 0.0 copy-start.1
  3.4 0.0 copy-start.3
  3.4 17.9 %local_maps.1 = (bf16[4,8,128,512]{3,2,1,0:T(8,128)(2,1)}, bf16[4,8,128,512]{3,2,1,0:T(8,128)(2,1)}, f32[4,128,256]{2,1,0:T(8,128)S(1)}) custom-call(bf16[512,1024]{1,0:T(8,128)(2,1)S(1)} %copy-done, bf16[512,1024]{1,0:T(8,128)(2,1)S(1)} %copy-done.2, f32[4,8,128]{2,1,0:T(8,128)S(1)} %reshape.13.b_ref), custom_call_target="tpu_custom_call" | custom-call | tf_op jit(solution)/shard_map/local_maps/pallas_call | solution.py:121
  21.3 1.7 %collective-permute-start = (f32[128,256]{1,0:T(8,128)S(1)}, f32[128,256]{1,0:T(8,128)S(1)}, u32[]{:S(2)}, u32[]{:S(2)}) collective-permute-start(f32[128,256]{1,0:T(8,128)S(1)} %get-tuple-element.27), channel_id=1, source_target_pairs={{0,8},{8,16},{16,24},{24,0},{32,40},{40,48},{48,56},{56,32},{64,72... | collective-permute-start | bytes 393224 | tf_op jit(solution)/shard_map/ppermute | solution.py:286
  23.0 2.9 %collective-permute-start.1 = (f32[128,256]{1,0:T(8,128)S(1)}, f32[128,256]{1,0:T(8,128)S(1)}, u32[]{:S(2)}, u32[]{:S(2)}) collective-permute-start(f32[128,256]{1,0:T(8,128)S(1)} %get-tuple-element.26), channel_id=1, source_target_pairs={{0,16},{8,24},{16,0},{24,8},{32,48},{40,56},{48,32},{56,40},{64,80... | collective-permute-start | bytes 393224 | tf_op jit(solution)/shard_map/ppermute | solution.py:286
  25.9 1.3 %collective-permute-start.2 = (f32[128,256]{1,0:T(8,128)S(1)}, f32[128,256]{1,0:T(8,128)S(1)}, u32[]{:S(2)}, u32[]{:S(2)}) collective-permute-start(f32[128,256]{1,0:T(8,128)S(1)} %get-tuple-element.25), channel_id=1, source_target_pairs={{0,24},{8,0},{16,8},{24,16},{32,56},{40,32},{48,40},{56,48},{64,88... | collective-permute-start | bytes 393224 | tf_op jit(solution)/shard_map/ppermute | solution.py:286
  27.2 0.1 pad_add_fusion.me_ref
  27.3 0.6 collective-permute-done.r1
  27.9 4.0 %collective-permute-done.1.r2 = f32[128,256]{1,0:T(8,128)S(1)} collective-permute-done((f32[128,256]{1,0:T(8,128)S(1)}, f32[128,256]{1,0:T(8,128)S(1)}, u32[]{:S(2)}, u32[]{:S(2)}) %collective-permute-start.1) | collective-permute-done | bytes 131104 | tf_op jit(solution)/shard_map/ppermute | solution.py:286
  31.9 0.0 collective-permute-done.2.r3
  31.9 1.1 %row_maps.1 = (f32[3,128,256]{2,1,0:T(8,128)S(1)}, f32[128,256]{1,0:T(8,128)S(1)}) custom-call(s32[2]{0:T(128)S(1)} %pad_add_fusion.me_ref, f32[4,128,256]{2,1,0:T(8,128)S(1)} %get-tuple-element.15.own_ref, f32[128,256]{1,0:T(8,128)S(1)} %collective-permute-done.r1, f32[128,256]{1,0:T(8,128)S(1)} %collective-permute-done.1.r2, ...), custom_call_target="tpu_custom_call" | custom-call | tf_op jit(solution)/shard_map/row_maps/pallas_call | solution.py:290
  33.1 2.0 %collective-permute-start.3 = (f32[128,256]{1,0:T(8,128)S(1)}, f32[128,256]{1,0:T(8,128)S(1)}, u32[]{:S(2)}, u32[]{:S(2)}) collective-permute-start(f32[128,256]{1,0:T(8,128)S(1)} %get-tuple-element.16.own_ref), channel_id=1, source_target_pairs={{0,32},{8,40},{16,48},{24,56},{32,64},{40,72},{48,80},{56,88},{64,... | collective-permute-start | bytes 393224 | tf_op jit(solution)/shard_map/ppermute | solution.py:293
  35.0 1.5 %collective-permute-start.4 = (f32[128,256]{1,0:T(8,128)S(1)}, f32[128,256]{1,0:T(8,128)S(1)}, u32[]{:S(2)}, u32[]{:S(2)}) collective-permute-start(f32[128,256]{1,0:T(8,128)S(1)} %get-tuple-element.16.own_ref), channel_id=1, source_target_pairs={{0,64},{8,72},{16,80},{24,88},{32,96},{40,104},{48,112},{56,120},{... | collective-permute-start | bytes 393224 | tf_op jit(solution)/shard_map/ppermute | solution.py:293
  36.5 1.9 %collective-permute-start.5 = (f32[128,256]{1,0:T(8,128)S(1)}, f32[128,256]{1,0:T(8,128)S(1)}, u32[]{:S(2)}, u32[]{:S(2)}) collective-permute-start(f32[128,256]{1,0:T(8,128)S(1)} %get-tuple-element.16.own_ref), channel_id=1, source_target_pairs={{0,96},{8,104},{16,112},{24,120},{32,0},{40,8},{48,16},{56,24},{64... | collective-permute-start | bytes 393224 | tf_op jit(solution)/shard_map/ppermute | solution.py:293
  38.4 5.6 %collective-permute-done.3.r1 = f32[128,256]{1,0:T(8,128)S(1)} collective-permute-done((f32[128,256]{1,0:T(8,128)S(1)}, f32[128,256]{1,0:T(8,128)S(1)}, u32[]{:S(2)}, u32[]{:S(2)}) %collective-permute-start.3) | collective-permute-done | bytes 131104 | tf_op jit(solution)/shard_map/ppermute | solution.py:293
  44.0 1.4 %collective-permute-done.4.r2 = f32[128,256]{1,0:T(8,128)S(1)} collective-permute-done((f32[128,256]{1,0:T(8,128)S(1)}, f32[128,256]{1,0:T(8,128)S(1)}, u32[]{:S(2)}, u32[]{:S(2)}) %collective-permute-start.4) | collective-permute-done | bytes 131104 | tf_op jit(solution)/shard_map/ppermute | solution.py:293
  45.4 2.0 %collective-permute-done.5.r3 = f32[128,256]{1,0:T(8,128)S(1)} collective-permute-done((f32[128,256]{1,0:T(8,128)S(1)}, f32[128,256]{1,0:T(8,128)S(1)}, u32[]{:S(2)}, u32[]{:S(2)}) %collective-permute-start.5) | collective-permute-done | bytes 131104 | tf_op jit(solution)/shard_map/ppermute | solution.py:293
  47.5 0.0 copy-done.4
  47.5 1.4 %plane_maps.1 = (f32[128,256]{1,0:T(8,128)S(1)}, f32[128,128]{1,0:T(8,128)S(1)}, f32[128,128]{1,0:T(8,128)S(1)}) custom-call(s32[2]{0:T(128)S(1)} %pad_add_fusion.me_ref, f32[128,256]{1,0:T(8,128)S(1)} %get-tuple-element.16.own_ref, f32[128,256]{1,0:T(8,128)S(1)} %collective-permute-done.3.r1, f32[128,256]{1,0:T(8,128)S(1)} %collective-permute-done.4.r2, ...), custom_call_target="tpu_custom_call" | custom-call | tf_op jit(solution)/shard_map/plane_maps/pallas_call | solution.py:294
  48.9 7.9 %collective-permute-start.6 = (f32[128,128]{1,0:T(8,128)S(1)}, f32[128,128]{1,0:T(8,128)S(1)}, u32[]{:S(2)}, u32[]{:S(2)}) collective-permute-start(f32[128,128]{1,0:T(8,128)S(1)} %get-tuple-element.18), channel_id=1, source_target_pairs={{0,128},{8,136},{16,144},{24,152},{32,160},{40,168},{48,176},{56,1... | collective-permute-start | bytes 196616 | tf_op jit(solution)/shard_map/ppermute | solution.py:301
  56.8 1.9 %collective-permute-done.6.mid_ref = f32[128,128]{1,0:T(8,128)S(1)} collective-permute-done((f32[128,128]{1,0:T(8,128)S(1)}, f32[128,128]{1,0:T(8,128)S(1)}, u32[]{:S(2)}, u32[]{:S(2)}) %collective-permute-start.6) | collective-permute-done | bytes 65568 | tf_op jit(solution)/shard_map/ppermute | solution.py:301
  58.7 1.0 %states.1.s_own = f32[4,128,128]{2,1,0:T(8,128)S(1)} custom-call(s32[2]{0:T(128)S(1)} %pad_add_fusion.me_ref, f32[128,128]{1,0:T(8,128)S(1)} %get-tuple-element.17.s0t_ref, f32[128,128]{1,0:T(8,128)S(1)} %collective-permute-done.6.mid_ref, f32[128,256]{1,0:T(8,128)S(1)} %get-tuple-element.19.pre_ref, f32[3,128,256]{2,1,0:T(8,128)S(1)} %get-tuple-element.20.rows_ref), custom_call_target="tpu_custom_call" | custom-call | tf_op jit(solution)/shard_map/states/pallas_call | solution.py:302
  59.7 1.4 %collective-permute-start.7 = (f32[128,128]{1,0:T(8,128)S(1)}, f32[128,128]{1,0:T(8,128)S(1)}, u32[]{:S(2)}, u32[]{:S(2)}) collective-permute-start(f32[128,128]{1,0:T(8,128)S(1)} %get-tuple-element.30), channel_id=1, source_target_pairs={{0,8},{8,16},{16,24},{24,0},{32,40},{40,48},{48,56},{56,32},{64,72... | collective-permute-start | bytes 196616 | tf_op jit(solution)/shard_map/ppermute | solution.py:286
  61.0 2.6 %collective-permute-start.8 = (f32[128,128]{1,0:T(8,128)S(1)}, f32[128,128]{1,0:T(8,128)S(1)}, u32[]{:S(2)}, u32[]{:S(2)}) collective-permute-start(f32[128,128]{1,0:T(8,128)S(1)} %get-tuple-element.29), channel_id=1, source_target_pairs={{0,16},{8,24},{16,0},{24,8},{32,48},{40,56},{48,32},{56,40},{64,80... | collective-permute-start | bytes 196616 | tf_op jit(solution)/shard_map/ppermute | solution.py:286
  63.6 0.8 collective-permute-start.9
  64.4 0.0 copy-done.1
  64.4 0.0 copy-done.3
  64.4 0.0 copy-start.5
  64.4 8.9 %local_outputs.1 = (f32[4,512,128]{2,1,0:T(8,128)S(1)}, f32[4,512,128]{2,1,0:T(8,128)S(1)}) custom-call(bf16[512,512]{1,0:T(8,128)(2,1)S(1)} %copy-done.3, bf16[512,1024]{1,0:T(8,128)(2,1)S(1)} %copy-done.1, bf16[4,8,128,512]{3,2,1,0:T(8,128)(2,1)} %get-tuple-element.21.wu_ref, bf16[4,8,128,512]{3,2,1,0:T(8,128)(2,1)} %get-tuple-element.22.r_ref), custom_call_target="tpu_custom_call" | custom-call | flops 1073741824 | bytes 12582912 | tf_op jit(solution)/shard_map/local_outputs/pallas_call | solution.py:168
  73.3 0.0 collective-permute-done.7.s1
  73.3 0.0 collective-permute-done.8.s2
  73.3 0.0 collective-permute-done.9.s3
  73.3 0.0 copy-done.5
  73.3 1.1 %finish.1 = bf16[512,512]{1,0:T(8,128)(2,1)S(1)} custom-call(s32[2]{0:T(128)S(1)} %pad_add_fusion.me_ref, f32[4,128,128]{2,1,0:T(8,128)S(1)} %states.1.s_own, f32[128,128]{1,0:T(8,128)S(1)} %collective-permute-done.7.s1, f32[128,128]{1,0:T(8,128)S(1)} %collective-permute-done.8.s2, f32[128,128]{1,0:T(8,128)S(1)} %collective-permute-done.9.s3, ...), custom_call_target="tpu_custom_call" | custom-call | tf_op jit(solution)/shard_map/finish/pallas_call | solution.py:304
  74.5 14.6 %all_to_all.19 = bf16[8,64,512]{2,1,0:T(8,128)(2,1)S(1)} all-to-all(bf16[8,64,512]{2,1,0:T(8,128)(2,1)S(1)} %bitcast.24), channel_id=1, replica_groups=mesh['ctx'=32,'head'=8] {'head'}, dimensions={0} | all-to-all | bytes 1048576 | tf_op jit(solution)/shard_map/all_to_all | solution.py:307
  89.1 0.8 copy.9
  (3 shorter events, 0.1 us)
Async XLA Ops:
  0.0 47.5 %copy-start.4 = (f32[4,128,128]{2,1,0:T(8,128)S(1)}, f32[4,128,128]{2,1,0:T(8,128)}, u32[]{:S(2)}) copy-start(f32[4,128,128]{2,1,0:T(8,128)} %s0_ref.1) | copy-start | bytes 786436
  0.9 1.2 %copy-start = (bf16[512,1024]{1,0:T(8,128)(2,1)S(1)}, bf16[512,1024]{1,0:T(8,128)(2,1)}, u32[]{:S(2)}) copy-start(bf16[512,1024]{1,0:T(8,128)(2,1)} %k_ref.3) | copy-start | bytes 3145732
  2.2 1.2 %copy-start.2 = (bf16[512,1024]{1,0:T(8,128)(2,1)S(1)}, bf16[512,1024]{1,0:T(8,128)(2,1)}, u32[]{:S(2)}) copy-start(bf16[512,1024]{1,0:T(8,128)(2,1)} %v_ref.1) | copy-start | bytes 3145732
  3.4 61.0 %copy-start.1 = (bf16[512,1024]{1,0:T(8,128)(2,1)S(1)}, bf16[512,1024]{1,0:T(8,128)(2,1)}, u32[]{:S(2)}) copy-start(bf16[512,1024]{1,0:T(8,128)(2,1)} %k_ref.3) | copy-start | bytes 3145732
  3.4 61.0 %copy-start.3 = (bf16[512,512]{1,0:T(8,128)(2,1)S(1)}, bf16[512,512]{1,0:T(8,128)(2,1)}, u32[]{:S(2)}) copy-start(bf16[512,512]{1,0:T(8,128)(2,1)} %q_ref.1) | copy-start | bytes 1572868
  21.3 6.6 %collective-permute-start = (f32[128,256]{1,0:T(8,128)S(1)}, f32[128,256]{1,0:T(8,128)S(1)}, u32[]{:S(2)}, u32[]{:S(2)}) collective-permute-start(f32[128,256]{1,0:T(8,128)S(1)} %get-tuple-element.27), channel_id=1, source_target_pairs={{0,8},{8,16},{16,24},{24,0},{32,40},{40,48},{48,56},{56,32},{64,72... | collective-permute-start | bytes 393224 | tf_op jit(solution)/shard_map/ppermute | solution.py:286
  23.0 9.0 %collective-permute-start.1 = (f32[128,256]{1,0:T(8,128)S(1)}, f32[128,256]{1,0:T(8,128)S(1)}, u32[]{:S(2)}, u32[]{:S(2)}) collective-permute-start(f32[128,256]{1,0:T(8,128)S(1)} %get-tuple-element.26), channel_id=1, source_target_pairs={{0,16},{8,24},{16,0},{24,8},{32,48},{40,56},{48,32},{56,40},{64,80... | collective-permute-start | bytes 393224 | tf_op jit(solution)/shard_map/ppermute | solution.py:286
  25.9 6.0 %collective-permute-start.2 = (f32[128,256]{1,0:T(8,128)S(1)}, f32[128,256]{1,0:T(8,128)S(1)}, u32[]{:S(2)}, u32[]{:S(2)}) collective-permute-start(f32[128,256]{1,0:T(8,128)S(1)} %get-tuple-element.25), channel_id=1, source_target_pairs={{0,24},{8,0},{16,8},{24,16},{32,56},{40,32},{48,40},{56,48},{64,88... | collective-permute-start | bytes 393224 | tf_op jit(solution)/shard_map/ppermute | solution.py:286
  33.1 10.9 %collective-permute-start.3 = (f32[128,256]{1,0:T(8,128)S(1)}, f32[128,256]{1,0:T(8,128)S(1)}, u32[]{:S(2)}, u32[]{:S(2)}) collective-permute-start(f32[128,256]{1,0:T(8,128)S(1)} %get-tuple-element.16.own_ref), channel_id=1, source_target_pairs={{0,32},{8,40},{16,48},{24,56},{32,64},{40,72},{48,80},{56,88},{64,... | collective-permute-start | bytes 393224 | tf_op jit(solution)/shard_map/ppermute | solution.py:293
  35.0 10.4 %collective-permute-start.4 = (f32[128,256]{1,0:T(8,128)S(1)}, f32[128,256]{1,0:T(8,128)S(1)}, u32[]{:S(2)}, u32[]{:S(2)}) collective-permute-start(f32[128,256]{1,0:T(8,128)S(1)} %get-tuple-element.16.own_ref), channel_id=1, source_target_pairs={{0,64},{8,72},{16,80},{24,88},{32,96},{40,104},{48,112},{56,120},{... | collective-permute-start | bytes 393224 | tf_op jit(solution)/shard_map/ppermute | solution.py:293
  36.5 10.9 %collective-permute-start.5 = (f32[128,256]{1,0:T(8,128)S(1)}, f32[128,256]{1,0:T(8,128)S(1)}, u32[]{:S(2)}, u32[]{:S(2)}) collective-permute-start(f32[128,256]{1,0:T(8,128)S(1)} %get-tuple-element.16.own_ref), channel_id=1, source_target_pairs={{0,96},{8,104},{16,112},{24,120},{32,0},{40,8},{48,16},{56,24},{64... | collective-permute-start | bytes 393224 | tf_op jit(solution)/shard_map/ppermute | solution.py:293
  48.9 9.8 %collective-permute-start.6 = (f32[128,128]{1,0:T(8,128)S(1)}, f32[128,128]{1,0:T(8,128)S(1)}, u32[]{:S(2)}, u32[]{:S(2)}) collective-permute-start(f32[128,128]{1,0:T(8,128)S(1)} %get-tuple-element.18), channel_id=1, source_target_pairs={{0,128},{8,136},{16,144},{24,152},{32,160},{40,168},{48,176},{56,1... | collective-permute-start | bytes 196616 | tf_op jit(solution)/shard_map/ppermute | solution.py:301
  59.7 13.6 %collective-permute-start.7 = (f32[128,128]{1,0:T(8,128)S(1)}, f32[128,128]{1,0:T(8,128)S(1)}, u32[]{:S(2)}, u32[]{:S(2)}) collective-permute-start(f32[128,128]{1,0:T(8,128)S(1)} %get-tuple-element.30), channel_id=1, source_target_pairs={{0,8},{8,16},{16,24},{24,0},{32,40},{40,48},{48,56},{56,32},{64,72... | collective-permute-start | bytes 196616 | tf_op jit(solution)/shard_map/ppermute | solution.py:286
  61.0 12.2 %collective-permute-start.8 = (f32[128,128]{1,0:T(8,128)S(1)}, f32[128,128]{1,0:T(8,128)S(1)}, u32[]{:S(2)}, u32[]{:S(2)}) collective-permute-start(f32[128,128]{1,0:T(8,128)S(1)} %get-tuple-element.29), channel_id=1, source_target_pairs={{0,16},{8,24},{16,0},{24,8},{32,48},{40,56},{48,32},{56,40},{64,80... | collective-permute-start | bytes 196616 | tf_op jit(solution)/shard_map/ppermute | solution.py:286
  63.6 9.7 %collective-permute-start.9 = (f32[128,128]{1,0:T(8,128)S(1)}, f32[128,128]{1,0:T(8,128)S(1)}, u32[]{:S(2)}, u32[]{:S(2)}) collective-permute-start(f32[128,128]{1,0:T(8,128)S(1)} %get-tuple-element.28), channel_id=1, source_target_pairs={{0,24},{8,0},{16,8},{24,16},{32,56},{40,32},{48,40},{56,48},{64,88... | collective-permute-start | bytes 196616 | tf_op jit(solution)/shard_map/ppermute | solution.py:286
  64.4 8.9 %copy-start.5 = (f32[512]{0:T(512)S(1)}, f32[512]{0:T(512)}, u32[]{:S(2)}) copy-start(f32[512]{0:T(512)} %param.11) | copy-start | bytes 6148

commit v2 on v1

v2 whole, which is shorter than its diff:
```python
import functools
import jax
import jax.numpy as jnp
from jax import lax
from jax.experimental import pallas as pl
from jax.experimental.pallas import tpu as pltpu
from jax.sharding import PartitionSpec as P

D = 128
HALF = 64
ITEMS = 128
BLOCKS = 8
HEADS = 4
NY = 4
NZ = 8
F32 = jnp.float32
BF16 = jnp.bfloat16
VMEM_LIMIT = 48 * 1024 * 1024
OUTPUTS_LIMIT = 48 * 1024 * 1024
SMALL_LIMIT = 16 * 1024 * 1024
PER = 2


def split(x):
    hi = x.astype(BF16)
    lo = (x - hi.astype(F32)).astype(BF16)
    return hi, lo


def mm(a, b):
    return lax.dot_general(a, b, (((1,), (0,)), ((), ())), preferred_element_type=F32)


def mm_nt(a, b):
    return lax.dot_general(a, b, (((1,), (1,)), ((), ())), preferred_element_type=F32)


def mm_tn(a, b):
    return lax.dot_general(a, b, (((0,), (0,)), ((), ())), preferred_element_type=F32)


def both(parts, axis):
    return jnp.concatenate(parts, axis)


def narrow3(ah, al, bh, bl):
    right = both([bh, bl], 1)
    out = mm(both([ah, al], 1), both([right, right], 0))
    return out[:, :D] + out[:, D:]


def wide3(ah, al, bh, bl):
    return mm(both([ah, al], 1), both([bh, bh], 0)) + mm(ah, bl)


def join(early, late):
    out = wide3(*split(late[:, :D]), *split(early))
    return both([out[:, :D], out[:, D:] + late[:, D:]], 1)


def order(shape, axis):
    place = lax.broadcasted_iota(jnp.int32, shape, axis)
    return 2 * (place % HALF) + place // HALF


def block_keys(ref, h, b):
    rows = slice(b * HALF, (b + 1) * HALF)
    return both([ref[rows, 2 * h * D : (2 * h + 1) * D], ref[rows, (2 * h + 1) * D : (2 * h + 2) * D]], 0)


def stacked3(ah, al, bh, bl):
    rows = ah.shape[0]
    out = mm(both([ah, al], 0), both([bh, bl], 1))
    return out[:rows, :D] + out[:rows, D:] + out[rows:, :D]


def late_rows(x, width):
    return both([x[i : i + width] for i in range(width, ITEMS, 2 * width)], 0)


def drop_late(x, y, width):
    parts = []
    for n, i in enumerate(range(0, ITEMS, 2 * width)):
        parts += [x[i : i + width], x[i + width : i + 2 * width] - y[n * width : (n + 1) * width]]
    return both(parts, 0)


def item_betas(b_rows):
    left = lax.broadcasted_iota(jnp.int32, (1, ITEMS), 1) < HALF
    rows = []
    for h in range(PER):
        pair = [b_rows[pl.ds((pl.program_id(0) * PER + h) * 2 + j, 1), :] for j in range(2)]
        for c in range(BLOCKS // 2):
            lanes = slice(c * ITEMS, (c + 1) * ITEMS)
            first, second = pair[0][:, lanes], pair[1][:, lanes]
            rows.append(jnp.where(left, first, pltpu.roll(second, HALF, 1)))
            rows.append(jnp.where(left, pltpu.roll(first, HALF, 1), second))
    return both(rows, 0)


def local_maps_kernel(k_ref, v_ref, b_ref, wu_ref, r_ref, tot_ref):
    shape = (ITEMS, ITEMS)
    ni, nj = order(shape, 0), order(shape, 1)
    eye = (ni == nj).astype(F32)
    masks = []
    for level in range(7):
        hit = ((ni >> (level + 1)) == (nj >> (level + 1))) & ((ni >> level) > (nj >> level))
        masks.append(hit.astype(F32))
    low = [m.astype(BF16) for m in masks]
    units = [(h, b) for h in range(PER) for b in range(BLOCKS)]
    keys = [block_keys(k_ref, h, b) for h, b in units]
    grams = [mm_nt(k, k) for k in keys]
    squares = both([jnp.sum(g * eye, 0, keepdims=True) for g in grams], 0)
    pairs = both([jnp.sum(g * masks[0], 0, keepdims=True) for g in grams], 0)
    rk = lax.rsqrt(squares + 1e-06)
    beta_rk = item_betas(b_ref) * rk
    beta_rk2 = beta_rk * rk
    pairs = pairs * pltpu.roll(beta_rk2, HALF, 1)
    columns = beta_rk2.T
    pair_columns = pairs.T
    inv, pieces = [], []
    for i, g in enumerate(grams):
        l = columns[:, i : i + 1] * g
        x = l * masks[1]
        x = both([x[:HALF], x[HALF:] - pair_columns[:HALF, i : i + 1] * x[:HALF]], 0)
        x = x - pltpu.roll(x, HALF, 1) * pairs[i : i + 1]
        inv.append(eye - l * masks[0] - x)
        pieces.append(split(l))
    for level in range(2, 7):
        m = low[level]
        width = 1 << (level - 1)
        cut = [split(t) for t in inv]
        if width >= 8:
            left = [split(late_rows(t, width)) for t in inv] if width < 16 else [(late_rows(c[0], width), late_rows(c[1], width)) for c in cut]
        else:
            left = cut
        prod = stacked3 if width >= 8 else narrow3
        step = [prod(*t, p[0] * m, p[1] * m) for t, p in zip(left, pieces)]
        step = [prod(*split(x), *c) for x, c in zip(step, cut)]
        if width >= 8:
            inv = [drop_late(t, x, width) for t, x in zip(inv, step)]
        else:
            inv = [t - x for t, x in zip(inv, step)]
    maps = []
    for i, (h, b) in enumerate(units):
        v = block_keys(v_ref, h, b)
        w = mm(both(split(inv[i] * beta_rk2[i : i + 1]), 1), both([keys[i], keys[i]], 0))
        u = mm(both(split(inv[i] * beta_rk[i : i + 1]), 1), both([v, v], 0))
        wh, wl = split(w)
        uh, ul = split(u)
        wu = both([wh, uh, wl, ul], 1)
        wu_ref[h, b] = wu
        r = mm_tn(keys[i], wu)
        r = r[:, : 2 * D] + r[:, 2 * D :]
        maps.append(both([eye - r[:, :D], r[:, D:]], 1))

    def keep(h, b, m):
        hi, lo = split(m)
        r_ref[h, b - 1] = both([hi, lo], 1)

    two = [join(maps[i], maps[i + 1]) for i in range(0, len(maps), 2)]
    four = [join(two[i], two[i + 1]) for i in range(0, len(two), 2)]
    for h in range(PER):
        m, t, f = maps[h * 8 :], two[h * 4 :], four[h * 2 :]
        for b, node in ((1, m[0]), (2, t[0]), (3, m[2]), (4, f[0]), (5, m[4]), (6, t[2]), (7, m[6])):
            keep(h, b, node)
        tot_ref[h] = join(f[0], f[1])


def local_maps(keys, values, betas):
    return pl.pallas_call(
        local_maps_kernel,
        grid=(HEADS // PER,),
        in_specs=[
            pl.BlockSpec((BLOCKS * HALF, PER * 2 * D), lambda h: (0, h)),
            pl.BlockSpec((BLOCKS * HALF, PER * 2 * D), lambda h: (0, h)),
            pl.BlockSpec((2 * HEADS, BLOCKS * HALF), lambda h: (0, 0)),
        ],
        out_specs=[
            pl.BlockSpec((PER, BLOCKS, ITEMS, 4 * D), lambda h: (h, 0, 0, 0)),
            pl.BlockSpec((PER, BLOCKS - 1, D, 4 * D), lambda h: (h, 0, 0, 0)),
            pl.BlockSpec((PER, D, 2 * D), lambda h: (h, 0, 0)),
        ],
        out_shape=[
            jax.ShapeDtypeStruct((HEADS, BLOCKS, ITEMS, 4 * D), BF16),
            jax.ShapeDtypeStruct((HEADS, BLOCKS - 1, D, 4 * D), BF16),
            jax.ShapeDtypeStruct((HEADS, D, 2 * D), F32),
        ],
        compiler_params=pltpu.CompilerParams(vmem_limit_bytes=VMEM_LIMIT),
        name="local_maps",
    )(keys, values, betas)


def outputs_kernel(q_ref, k_ref, wu_ref, r_ref, qe_ref, ol_ref):
    shape = (HALF, ITEMS)
    seen = (
        lax.broadcasted_iota(jnp.int32, shape, 1) % HALF <= lax.broadcasted_iota(jnp.int32, shape, 0)
    ).astype(F32)
    node = [None] + [(r_ref[0, b][:, : 2 * D], r_ref[0, b][:, 2 * D :]) for b in range(BLOCKS - 1)]

    def onto(early, late):
        out = wide3(late[0][:, :D], late[1][:, :D], *early)
        added = late[0][:, D:].astype(F32) + late[1][:, D:].astype(F32)
        return split(both([out[:, :D], out[:, D:] + added], 1))

    prefix = list(node)
    prefix[3] = onto(node[2], node[3])
    prefix[5] = onto(node[4], node[5])
    prefix[6] = onto(node[4], node[6])
    prefix[7] = onto(prefix[6], node[7])
    for b in range(BLOCKS):
        rows = slice(b * HALF, (b + 1) * HALF)
        q = q_ref[rows, :]
        qf = q.astype(F32)
        sh, sl = split(mm_nt(q, block_keys(k_ref, 0, b)) * seen)
        wu = wu_ref[0, b]
        x = wide3(sh, sl, wu[:, : 2 * D], wu[:, 2 * D :])
        qe, ol = qf - x[:, :D], x[:, D:]
        if b:
            e = wide3(*split(qe), *prefix[b])
            qe, ol = e[:, :D], e[:, D:] + ol
        rq = lax.rsqrt(jnp.sum(qf * qf, -1, keepdims=True) + 1e-06)
        qe_ref[0, rows, :] = qe * rq
        ol_ref[0, rows, :] = ol * rq


def local_outputs(queries, keys, wu, prefixes):
    flops = 2 * HEADS * BLOCKS * HALF * D * D * 16
    return pl.pallas_call(
        outputs_kernel,
        grid=(HEADS,),
        in_specs=[
            pl.BlockSpec((BLOCKS * HALF, D), lambda h: (0, h)),
            pl.BlockSpec((BLOCKS * HALF, 2 * D), lambda h: (0, h)),
            pl.BlockSpec((1, BLOCKS, ITEMS, 4 * D), lambda h: (h, 0, 0, 0)),
            pl.BlockSpec((1, BLOCKS - 1, D, 4 * D), lambda h: (h, 0, 0, 0)),
        ],
        out_specs=[
            pl.BlockSpec((1, BLOCKS * HALF, D), lambda h: (h, 0, 0)),
            pl.BlockSpec((1, BLOCKS * HALF, D), lambda h: (h, 0, 0)),
        ],
        out_shape=[jax.ShapeDtypeStruct((HEADS, BLOCKS * HALF, D), F32)] * 2,
        compiler_params=pltpu.CompilerParams(vmem_limit_bytes=OUTPUTS_LIMIT),
        cost_estimate=pl.CostEstimate(flops=flops, bytes_accessed=12 * 1024 * 1024, transcendentals=0),
        name="local_outputs",
    )(queries, keys, wu, prefixes)


def in_vmem(n):
    return [pl.BlockSpec(memory_space=pltpu.VMEM)] * n


def in_smem():
    return [pl.BlockSpec(memory_space=pltpu.SMEM)]


def row_maps_kernel(me_ref, own_ref, r1, r2, r3, pre_ref, tot_ref, held):
    y = me_ref[0]
    held[y] = own_ref[...]
    for s, ref in ((1, r1), (2, r2), (3, r3)):
        held[(y + NY - s) % NY] = ref[...]
    two = join(held[0], held[1])
    pre_ref[0] = held[0]
    pre_ref[1] = two
    pre_ref[2] = join(two, held[2])
    tot_ref[...] = join(two, join(held[2], held[3]))


def plane_maps_kernel(me_ref, own_ref, r1, r2, r3, s0_ref, pre_ref, end_ref, s0t_ref, held):
    y, z = me_ref[0], me_ref[1] % 4
    held[z] = own_ref[...]
    for s, ref in ((1, r1), (2, r2), (3, r3)):
        held[(z + 4 - s) % 4] = ref[...]
    start = s0_ref[y].T
    s0t_ref[...] = start
    two = join(held[0], held[1])
    prefixes = (held[0], two, join(two, held[2]))
    pre_ref[...] = prefixes[0]
    for i in (2, 3):

        @pl.when(z == i)
        def _():
            pre_ref[...] = prefixes[i - 1]

    end_ref[...] = apply(join(held[2], held[3]), apply(two, start))


def apply(m, state):
    return narrow3(*split(m[:, :D]), *split(state)) + m[:, D:]


def states_kernel(me_ref, s0t_ref, mid_ref, pre_ref, rows_ref, out_ref):
    z = me_ref[1]
    base = jnp.where(z >= 4, mid_ref[...], s0t_ref[...])
    state = jnp.where(z % 4 > 0, apply(pre_ref[...], base), base)
    out_ref[0] = state
    for i in range(1, NY):
        out_ref[i] = apply(rows_ref[i - 1], state)


def finish_kernel(me_ref, s_own, s1, s2, s3, qe_ref, ol_ref, g_ref, out_ref):
    y = me_ref[0]
    for s in range(NY):
        h = (y + NY - s) % NY
        state = (s_own, s1, s2, s3)[s][...]
        raw = narrow3(*split(qe_ref[h]), *split(state)) + ol_ref[h]
        scale = lax.rsqrt(jnp.mean(raw * raw, -1, keepdims=True) + 1e-06)
        out_ref[:, pl.ds(pl.multiple_of(h * D, D), D)] = (raw * scale * g_ref[h]).astype(BF16)


def call(kernel, n_in, out_shape, scratch=(), name=None):
    return pl.pallas_call(
        kernel,
        in_specs=in_smem() + in_vmem(n_in),
        out_specs=jax.tree.map(lambda _: pl.BlockSpec(memory_space=pltpu.VMEM), out_shape),
        out_shape=out_shape,
        scratch_shapes=list(scratch),
        compiler_params=pltpu.CompilerParams(vmem_limit_bytes=SMALL_LIMIT),
        name=name,
    )


def shift_y(s):
    return [(z * NY + y, z * NY + (y + s) % NY) for z in range(NZ) for y in range(NY)]


def shift_z(s):
    return [
        (z * NY + y, (z // 4 * 4 + (z % 4 + s) % 4) * NY + y) for z in range(NZ) for y in range(NY)
    ]


ACROSS = [(a * NY + y, b * NY + y) for a, b in zip(range(NZ), (7, 6, 5, 4, 3, 2, 1, 0)) for y in range(NY)]


def body(queries, keys, values, betas, initial_state, out_gain):
    f32 = lambda *shape: jax.ShapeDtypeStruct(shape, F32)
    place = lax.axis_index("ctx").astype(jnp.int32)
    y, z = place % NY, place // NY
    me = jnp.stack([y, z])
    wu, prefixes, total = local_maps(keys, values, betas.T)

    def exchange(array):
        mine = [lax.dynamic_index_in_dim(array, (y + s) % NY, 0, False) for s in range(NY)]
        return mine[:1] + [lax.ppermute(mine[s], "ctx", shift_y(s)) for s in (1, 2, 3)]

    rows_pre, row_total = call(
        row_maps_kernel, 4, [f32(3, D, 2 * D), f32(D, 2 * D)], [pltpu.VMEM((4, D, 2 * D), F32)], "row_maps"
    )(me, *exchange(total))
    others = [lax.ppermute(row_total, "ctx", shift_z(s)) for s in (1, 2, 3)]
    qe, ol = local_outputs(queries, keys, wu, prefixes)
    others, qe, ol = lax.optimization_barrier((others, qe, ol))
    plane_pre, end, start = call(
        plane_maps_kernel,
        5,
        [f32(D, 2 * D), f32(D, D), f32(D, D)],
        [pltpu.VMEM((4, D, 2 * D), F32)],
        "plane_maps",
    )(me, row_total, *others, initial_state)
    mid = lax.ppermute(end, "ctx", ACROSS)
    states = call(states_kernel, 4, f32(NY, D, D), (), "states")(me, start, mid, plane_pre, rows_pre)
    local_out = call(
        finish_kernel, 7, jax.ShapeDtypeStruct((BLOCKS * HALF, HEADS * D), BF16), (), "finish"
    )(me, *exchange(states), qe, ol, out_gain.reshape(HEADS, 1, D))
    return lax.all_to_all(local_out, "head", split_axis=0, concat_axis=1, tiled=True)


def solution(mesh):
    placed = (
        P("ctx", "head"),
        P("ctx", "head"),
        P("ctx", "head"),
        P("ctx", "head"),
        P("head", None, None),
        P("head"),
    )
    return jax.shard_map(
        body, mesh=mesh, in_specs=placed, out_specs=P(("ctx", "head"), None), check_vma=False
    )
```

time: 90.4 us -> 81.1 us (0.90)
  starting transfers between devices: 23.9 us -> 17.3 us
  Pallas kernels: 31.4 us -> 27.9 us
    ppermute x3, waiting for transfers between devices: 9.01 us -> 0.01 us  [body(): others = [lax.ppermute(row_total, 'ctx', shift_z(s)) for s in (1, 2, 3)]]
    ppermute x6, waiting for transfers between devices: 4.63 us -> 12.6 us  [exchange(): lax.ppermute(mine[s], 'ctx', shift_y(s))]
    ppermute x6, starting transfers between devices: 10.6 us -> 6.82 us  [exchange(): lax.ppermute(mine[s], 'ctx', shift_y(s))]
    pallas_call x1, Pallas kernels: 17.9 us -> 14.1 us  [local_maps(): pl.pallas_call(local_maps_kernel, grid=(HEADS // PER,), in_specs=[pl.Bloc...]
    ppermute x1, starting transfers between devices: 7.91 us -> 4.23 us  [body(): mid = lax.ppermute(end, 'ctx', ACROSS)]
    unnamed x12 -> x14, local copies, waits for them, and re-layouts: 2.46 us -> 4.22 us
    ppermute x1, waiting for transfers between devices: 1.88 us -> 3.13 us  [body(): mid = lax.ppermute(end, 'ctx', ACROSS)]
    reshape x3 -> x0, local copies, waits for them, and re-layouts: 0.94 us -> none  [body(): betas.reshape(BLOCKS, HALF, HEADS, 2).transpose(2, 0, 3, 1)]
  transfers between devices with their start and end apart: 10 -> 10, of which waited for: 6 -> 7; matrix products, arithmetic and copies ran while one was open for 0% -> 0% of each run, Pallas kernels for 10% -> 12%
where the time goes in v2:
time: 81.1 us; the launch traced here: 80.8 us
  Pallas kernels  27.9 us (34%)
  starting transfers between devices  17.3 us (21%)
  waiting for transfers between devices  15.7 us (19%)
  blocking collectives  14.5 us (18%)
  local copies, waits for them, and re-layouts  5.12 us (6%)
    all_to_all x1, blocking collectives, body(): lax.all_to_all(local_out, 'head', split_axis=0, concat_axis=1, tiled=True)  14.5 us
    pallas_call x1, Pallas kernels, local_maps(): pl.pallas_call(local_maps_kernel, grid=(HEADS // PER,), in_specs=[pl.Bloc...  14.1 us
    ppermute x6, waiting for transfers between devices, exchange(): lax.ppermute(mine[s], 'ctx', shift_y(s))  12.6 us
    pallas_call x1, Pallas kernels, local_outputs(): pl.pallas_call(outputs_kernel, grid=(HEADS,), in_specs=[pl.BlockSpec((BLO...  9.34 us
    ppermute x6, starting transfers between devices, exchange(): lax.ppermute(mine[s], 'ctx', shift_y(s))  6.82 us
    ppermute x3, starting transfers between devices, body(): others = [lax.ppermute(row_total, 'ctx', shift_z(s)) for s in (1, 2, 3)]  6.27 us
    ppermute x1, starting transfers between devices, body(): mid = lax.ppermute(end, 'ctx', ACROSS)  4.23 us
    unnamed x14, local copies, waits for them, and re-layouts  4.22 us
  transfers between devices with their start and end apart: 10, of which 7 were waited for; matrix products, arithmetic and copies ran while one was open for 0% of the time, Pallas kernels for 12%

profile of v2, /device:TPU:32, one launch (start us, length us, event | category | flops | bytes accessed | tf_op | source)
XLA Modules:
  0.0 80.8 jit_solution(6236078382748811454)
XLA Ops:
  0.0 0.0 copy-start
  0.0 1.2 %copy-done = bf16[512,1024]{1,0:T(8,128)(2,1)S(1)} copy-done((bf16[512,1024]{1,0:T(8,128)(2,1)S(1)}, bf16[512,1024]{1,0:T(8,128)(2,1)}, u32[]{:S(2)}) %copy-start) | copy-done | bytes 1048600
  1.2 0.0 copy-start.2
  1.2 1.2 %copy-done.2 = bf16[512,1024]{1,0:T(8,128)(2,1)S(1)} copy-done((bf16[512,1024]{1,0:T(8,128)(2,1)S(1)}, bf16[512,1024]{1,0:T(8,128)(2,1)}, u32[]{:S(2)}) %copy-start.2) | copy-done | bytes 1048600
  2.5 0.0 copy-start.5
  2.5 0.7 copy-done.5
  3.2 0.0 copy-start.1
  3.2 14.1 %local_maps.1 = (bf16[4,8,128,512]{3,2,1,0:T(8,128)(2,1)}, bf16[4,7,128,512]{3,2,1,0:T(8,128)(2,1)}, f32[4,128,256]{2,1,0:T(8,128)S(1)}) custom-call(bf16[512,1024]{1,0:T(8,128)(2,1)S(1)} %copy-done, bf16[512,1024]{1,0:T(8,128)(2,1)S(1)} %copy-done.2, f32[8,512]{1,0:T(8,128)S(1)} %bitcast.25), custom_call_target="tpu_custom_call" | custom-call | tf_op jit(solution)/shard_map/local_maps/pallas_call | solution.py:171
  17.3 3.1 %collective-permute-start.2 = (f32[128,256]{1,0:T(8,128)S(1)}, f32[128,256]{1,0:T(8,128)S(1)}, u32[]{:S(2)}, u32[]{:S(2)}) collective-permute-start(f32[128,256]{1,0:T(8,128)S(1)} %get-tuple-element.35), channel_id=1, source_target_pairs={{0,24},{8,0},{16,8},{24,16},{32,56},{40,32},{48,40},{56,48},{64,88... | collective-permute-start | bytes 393224 | tf_op jit(solution)/shard_map/ppermute | solution.py:345
  20.4 0.6 collective-permute-start.1
  21.1 1.0 %collective-permute-start = (f32[128,256]{1,0:T(8,128)S(1)}, f32[128,256]{1,0:T(8,128)S(1)}, u32[]{:S(2)}, u32[]{:S(2)}) collective-permute-start(f32[128,256]{1,0:T(8,128)S(1)} %get-tuple-element.37), channel_id=1, source_target_pairs={{0,8},{8,16},{16,24},{24,0},{32,40},{40,48},{48,56},{56,32},{64,72... | collective-permute-start | bytes 393224 | tf_op jit(solution)/shard_map/ppermute | solution.py:345
  22.0 0.1 pad_add_fusion.me_ref
  22.1 3.9 %collective-permute-done.2.r3 = f32[128,256]{1,0:T(8,128)S(1)} collective-permute-done((f32[128,256]{1,0:T(8,128)S(1)}, f32[128,256]{1,0:T(8,128)S(1)}, u32[]{:S(2)}, u32[]{:S(2)}) %collective-permute-start.2) | collective-permute-done | bytes 131104 | tf_op jit(solution)/shard_map/ppermute | solution.py:345
  26.0 2.3 %collective-permute-done.1.r2 = f32[128,256]{1,0:T(8,128)S(1)} collective-permute-done((f32[128,256]{1,0:T(8,128)S(1)}, f32[128,256]{1,0:T(8,128)S(1)}, u32[]{:S(2)}, u32[]{:S(2)}) %collective-permute-start.1) | collective-permute-done | bytes 131104 | tf_op jit(solution)/shard_map/ppermute | solution.py:345
  28.3 1.4 %collective-permute-done.r1 = f32[128,256]{1,0:T(8,128)S(1)} collective-permute-done((f32[128,256]{1,0:T(8,128)S(1)}, f32[128,256]{1,0:T(8,128)S(1)}, u32[]{:S(2)}, u32[]{:S(2)}) %collective-permute-start) | collective-permute-done | bytes 131104 | tf_op jit(solution)/shard_map/ppermute | solution.py:345
  29.7 1.0 %row_maps.1 = (f32[3,128,256]{2,1,0:T(8,128)S(1)}, f32[128,256]{1,0:T(8,128)S(1)}) custom-call(s32[2]{0:T(128)S(1)} %pad_add_fusion.me_ref, f32[128,256]{1,0:T(8,128)S(1)} %get-tuple-element.38.own_ref, f32[128,256]{1,0:T(8,128)S(1)} %collective-permute-done.r1, f32[128,256]{1,0:T(8,128)S(1)} %collective-permute-done.1.r2, ...), custom_call_target="tpu_custom_call" | custom-call | tf_op jit(solution)/shard_map/row_maps/pallas_call | solution.py:347
  30.8 0.2 collective-permute-start.5
  30.9 3.3 %collective-permute-start.4 = (f32[128,256]{1,0:T(8,128)S(1)}, f32[128,256]{1,0:T(8,128)S(1)}, u32[]{:S(2)}, u32[]{:S(2)}) collective-permute-start(f32[128,256]{1,0:T(8,128)S(1)} %get-tuple-element.21.own_ref), channel_id=1, source_target_pairs={{0,64},{8,72},{16,80},{24,88},{32,96},{40,104},{48,112},{56,120},{... | collective-permute-start | bytes 393224 | tf_op jit(solution)/shard_map/ppermute | solution.py:350
  34.2 2.8 %collective-permute-start.3 = (f32[128,256]{1,0:T(8,128)S(1)}, f32[128,256]{1,0:T(8,128)S(1)}, u32[]{:S(2)}, u32[]{:S(2)}) collective-permute-start(f32[128,256]{1,0:T(8,128)S(1)} %get-tuple-element.21.own_ref), channel_id=1, source_target_pairs={{0,32},{8,40},{16,48},{24,56},{32,64},{40,72},{48,80},{56,88},{64,... | collective-permute-start | bytes 393224 | tf_op jit(solution)/shard_map/ppermute | solution.py:350
  37.0 0.0 copy-done.1
  37.0 0.0 copy-start.3
  37.0 1.0 %copy-done.3 = bf16[512,512]{1,0:T(8,128)(2,1)S(1)} copy-done((bf16[512,512]{1,0:T(8,128)(2,1)S(1)}, bf16[512,512]{1,0:T(8,128)(2,1)}, u32[]{:S(2)}) %copy-start.3) | copy-done | bytes 524312
  38.1 0.0 copy-start.4
  38.1 0.0 copy-start.6
  38.1 9.3 %local_outputs.1 = (f32[4,512,128]{2,1,0:T(8,128)S(1)}, f32[4,512,128]{2,1,0:T(8,128)S(1)}) custom-call(bf16[512,512]{1,0:T(8,128)(2,1)S(1)} %copy-done.3, bf16[512,1024]{1,0:T(8,128)(2,1)S(1)} %copy-done.1, bf16[4,8,128,512]{3,2,1,0:T(8,128)(2,1)} %get-tuple-element.22.wu_ref, bf16[4,7,128,512]{3,2,1,0:T(8,128)(2,1)} %get-tuple-element.23.r_ref), custom_call_target="tpu_custom_call" | custom-call | flops 1073741824 | bytes 12582912 | tf_op jit(solution)/shard_map/local_outputs/pallas_call | solution.py:229
  47.4 0.0 collective-permute-done.5.r3
  47.4 0.0 collective-permute-done.4.r2
  47.4 0.0 collective-permute-done.3.r1
  47.5 0.0 copy-done.4
  47.5 1.3 %plane_maps.1 = (f32[128,256]{1,0:T(8,128)S(1)}, f32[128,128]{1,0:T(8,128)S(1)}, f32[128,128]{1,0:T(8,128)S(1)}) custom-call(s32[2]{0:T(128)S(1)} %pad_add_fusion.me_ref, f32[128,256]{1,0:T(8,128)S(1)} %get-tuple-element.21.own_ref, f32[128,256]{1,0:T(8,128)S(1)} %collective-permute-done.3.r1, f32[128,256]{1,0:T(8,128)S(1)} %collective-permute-done.4.r2, ...), custom_call_target="tpu_custom_call" | custom-call | tf_op jit(solution)/shard_map/plane_maps/pallas_call | solution.py:353
  48.8 4.2 %collective-permute-start.6 = (f32[128,128]{1,0:T(8,128)S(1)}, f32[128,128]{1,0:T(8,128)S(1)}, u32[]{:S(2)}, u32[]{:S(2)}) collective-permute-start(f32[128,128]{1,0:T(8,128)S(1)} %get-tuple-element.30), channel_id=1, source_target_pairs={{0,224},{8,232},{16,240},{24,248},{32,192},{40,200},{48,208},{56,2... | collective-permute-start | bytes 196616 | tf_op jit(solution)/shard_map/ppermute | solution.py:360
  53.0 3.1 %collective-permute-done.6.mid_ref = f32[128,128]{1,0:T(8,128)S(1)} collective-permute-done((f32[128,128]{1,0:T(8,128)S(1)}, f32[128,128]{1,0:T(8,128)S(1)}, u32[]{:S(2)}, u32[]{:S(2)}) %collective-permute-start.6) | collective-permute-done | bytes 65568 | tf_op jit(solution)/shard_map/ppermute | solution.py:360
  56.2 0.9 %states.1 = f32[4,128,128]{2,1,0:T(8,128)S(1)} custom-call(s32[2]{0:T(128)S(1)} %pad_add_fusion.me_ref, f32[128,128]{1,0:T(8,128)S(1)} %get-tuple-element.29.s0t_ref, f32[128,128]{1,0:T(8,128)S(1)} %collective-permute-done.6.mid_ref, f32[128,256]{1,0:T(8,128)S(1)} %get-tuple-element.31.pre_ref, f32[3,128,256]{2,1,0:T(8,128)S(1)} %get-tuple-element.32.rows_ref), custom_call_target="tpu_custom_call" | custom-call | tf_op jit(solution)/shard_map/states/pallas_call | solution.py:361
  57.2 0.6 collective-permute-start.9
  57.8 0.6 collective-permute-start.8
  58.4 0.9 %collective-permute-start.7 = (f32[128,128]{1,0:T(8,128)S(1)}, f32[128,128]{1,0:T(8,128)S(1)}, u32[]{:S(2)}, u32[]{:S(2)}) collective-permute-start(f32[128,128]{1,0:T(8,128)S(1)} %get-tuple-element.41), channel_id=1, source_target_pairs={{0,8},{8,16},{16,24},{24,0},{32,40},{40,48},{48,56},{56,32},{64,72... | collective-permute-start | bytes 196616 | tf_op jit(solution)/shard_map/ppermute | solution.py:345
  59.3 2.2 %collective-permute-done.9.s3 = f32[128,128]{1,0:T(8,128)S(1)} collective-permute-done((f32[128,128]{1,0:T(8,128)S(1)}, f32[128,128]{1,0:T(8,128)S(1)}, u32[]{:S(2)}, u32[]{:S(2)}) %collective-permute-start.9) | collective-permute-done | bytes 65568 | tf_op jit(solution)/shard_map/ppermute | solution.py:345
  61.5 2.1 %collective-permute-done.8.s2 = f32[128,128]{1,0:T(8,128)S(1)} collective-permute-done((f32[128,128]{1,0:T(8,128)S(1)}, f32[128,128]{1,0:T(8,128)S(1)}, u32[]{:S(2)}, u32[]{:S(2)}) %collective-permute-start.8) | collective-permute-done | bytes 65568 | tf_op jit(solution)/shard_map/ppermute | solution.py:345
  63.6 0.7 collective-permute-done.7.s1
  64.3 0.0 copy-done.6
  64.3 1.1 %finish.1 = bf16[512,512]{1,0:T(8,128)(2,1)S(1)} custom-call(s32[2]{0:T(128)S(1)} %pad_add_fusion.me_ref, f32[128,128]{1,0:T(8,128)S(1)} %get-tuple-element.42.s_own, f32[128,128]{1,0:T(8,128)S(1)} %collective-permute-done.7.s1, f32[128,128]{1,0:T(8,128)S(1)} %collective-permute-done.8.s2, f32[128,128]{1,0:T(8,128)S(1)} %collective-permute-done.9.s3, ...), custom_call_target="tpu_custom_call" | custom-call | tf_op jit(solution)/shard_map/finish/pallas_call | solution.py:362
  65.4 14.5 %all_to_all.19 = bf16[8,64,512]{2,1,0:T(8,128)(2,1)S(1)} all-to-all(bf16[8,64,512]{2,1,0:T(8,128)(2,1)S(1)} %bitcast.24), channel_id=1, replica_groups=mesh['ctx'=32,'head'=8] {'head'}, dimensions={0} | all-to-all | bytes 1048576 | tf_op jit(solution)/shard_map/all_to_all | solution.py:365
  79.9 0.8 %copy.8 = bf16[8,8,8,512]{3,2,0,1:T(8,128)(2,1)} copy(bf16[8,8,8,512]{3,2,1,0:T(8,128)(2,1)S(1)} %bitcast.27) | data formatting | bytes 1048576 | tf_op jit(solution)/shard_map/all_to_all | solution.py:365
  (2 shorter events, 0.1 us)
Async XLA Ops:
  0.0 1.2 %copy-start = (bf16[512,1024]{1,0:T(8,128)(2,1)S(1)}, bf16[512,1024]{1,0:T(8,128)(2,1)}, u32[]{:S(2)}) copy-start(bf16[512,1024]{1,0:T(8,128)(2,1)} %k_ref.3) | copy-start | bytes 3145732
  1.2 1.2 %copy-start.2 = (bf16[512,1024]{1,0:T(8,128)(2,1)S(1)}, bf16[512,1024]{1,0:T(8,128)(2,1)}, u32[]{:S(2)}) copy-start(bf16[512,1024]{1,0:T(8,128)(2,1)} %v_ref.1) | copy-start | bytes 3145732
  2.5 0.7 copy-start.5
  3.2 33.9 %copy-start.1 = (bf16[512,1024]{1,0:T(8,128)(2,1)S(1)}, bf16[512,1024]{1,0:T(8,128)(2,1)}, u32[]{:S(2)}) copy-start(bf16[512,1024]{1,0:T(8,128)(2,1)} %k_ref.3) | copy-start | bytes 3145732
  17.3 8.7 %collective-permute-start.2 = (f32[128,256]{1,0:T(8,128)S(1)}, f32[128,256]{1,0:T(8,128)S(1)}, u32[]{:S(2)}, u32[]{:S(2)}) collective-permute-start(f32[128,256]{1,0:T(8,128)S(1)} %get-tuple-element.35), channel_id=1, source_target_pairs={{0,24},{8,0},{16,8},{24,16},{32,56},{40,32},{48,40},{56,48},{64,88... | collective-permute-start | bytes 393224 | tf_op jit(solution)/shard_map/ppermute | solution.py:345
  20.4 7.9 %collective-permute-start.1 = (f32[128,256]{1,0:T(8,128)S(1)}, f32[128,256]{1,0:T(8,128)S(1)}, u32[]{:S(2)}, u32[]{:S(2)}) collective-permute-start(f32[128,256]{1,0:T(8,128)S(1)} %get-tuple-element.36), channel_id=1, source_target_pairs={{0,16},{8,24},{16,0},{24,8},{32,48},{40,56},{48,32},{56,40},{64,80... | collective-permute-start | bytes 393224 | tf_op jit(solution)/shard_map/ppermute | solution.py:345
  21.1 8.6 %collective-permute-start = (f32[128,256]{1,0:T(8,128)S(1)}, f32[128,256]{1,0:T(8,128)S(1)}, u32[]{:S(2)}, u32[]{:S(2)}) collective-permute-start(f32[128,256]{1,0:T(8,128)S(1)} %get-tuple-element.37), channel_id=1, source_target_pairs={{0,8},{8,16},{16,24},{24,0},{32,40},{40,48},{48,56},{56,32},{64,72... | collective-permute-start | bytes 393224 | tf_op jit(solution)/shard_map/ppermute | solution.py:345
  30.8 16.7 %collective-permute-start.5 = (f32[128,256]{1,0:T(8,128)S(1)}, f32[128,256]{1,0:T(8,128)S(1)}, u32[]{:S(2)}, u32[]{:S(2)}) collective-permute-start(f32[128,256]{1,0:T(8,128)S(1)} %get-tuple-element.21.own_ref), channel_id=1, source_target_pairs={{0,96},{8,104},{16,112},{24,120},{32,0},{40,8},{48,16},{56,24},{64... | collective-permute-start | bytes 393224 | tf_op jit(solution)/shard_map/ppermute | solution.py:350
  30.9 16.5 %collective-permute-start.4 = (f32[128,256]{1,0:T(8,128)S(1)}, f32[128,256]{1,0:T(8,128)S(1)}, u32[]{:S(2)}, u32[]{:S(2)}) collective-permute-start(f32[128,256]{1,0:T(8,128)S(1)} %get-tuple-element.21.own_ref), channel_id=1, source_target_pairs={{0,64},{8,72},{16,80},{24,88},{32,96},{40,104},{48,112},{56,120},{... | collective-permute-start | bytes 393224 | tf_op jit(solution)/shard_map/ppermute | solution.py:350
  34.2 13.2 %collective-permute-start.3 = (f32[128,256]{1,0:T(8,128)S(1)}, f32[128,256]{1,0:T(8,128)S(1)}, u32[]{:S(2)}, u32[]{:S(2)}) collective-permute-start(f32[128,256]{1,0:T(8,128)S(1)} %get-tuple-element.21.own_ref), channel_id=1, source_target_pairs={{0,32},{8,40},{16,48},{24,56},{32,64},{40,72},{48,80},{56,88},{64,... | collective-permute-start | bytes 393224 | tf_op jit(solution)/shard_map/ppermute | solution.py:350
  37.0 1.0 %copy-start.3 = (bf16[512,512]{1,0:T(8,128)(2,1)S(1)}, bf16[512,512]{1,0:T(8,128)(2,1)}, u32[]{:S(2)}) copy-start(bf16[512,512]{1,0:T(8,128)(2,1)} %q_ref.1) | copy-start | bytes 1572868
  38.1 9.4 %copy-start.4 = (f32[4,128,128]{2,1,0:T(8,128)S(1)}, f32[4,128,128]{2,1,0:T(8,128)}, u32[]{:S(2)}) copy-start(f32[4,128,128]{2,1,0:T(8,128)} %s0_ref.1) | copy-start | bytes 786436
  38.1 26.2 %copy-start.6 = (f32[512]{0:T(512)S(1)}, f32[512]{0:T(512)}, u32[]{:S(2)}) copy-start(f32[512]{0:T(512)} %param.11) | copy-start | bytes 6148
  48.8 7.4 %collective-permute-start.6 = (f32[128,128]{1,0:T(8,128)S(1)}, f32[128,128]{1,0:T(8,128)S(1)}, u32[]{:S(2)}, u32[]{:S(2)}) collective-permute-start(f32[128,128]{1,0:T(8,128)S(1)} %get-tuple-element.30), channel_id=1, source_target_pairs={{0,224},{8,232},{16,240},{24,248},{32,192},{40,200},{48,208},{56,2... | collective-permute-start | bytes 196616 | tf_op jit(solution)/shard_map/ppermute | solution.py:360
  57.2 4.3 %collective-permute-start.9 = (f32[128,128]{1,0:T(8,128)S(1)}, f32[128,128]{1,0:T(8,128)S(1)}, u32[]{:S(2)}, u32[]{:S(2)}) collective-permute-start(f32[128,128]{1,0:T(8,128)S(1)} %get-tuple-element.39), channel_id=1, source_target_pairs={{0,24},{8,0},{16,8},{24,16},{32,56},{40,32},{48,40},{56,48},{64,88... | collective-permute-start | bytes 196616 | tf_op jit(solution)/shard_map/ppermute | solution.py:345
  57.8 5.8 %collective-permute-start.8 = (f32[128,128]{1,0:T(8,128)S(1)}, f32[128,128]{1,0:T(8,128)S(1)}, u32[]{:S(2)}, u32[]{:S(2)}) collective-permute-start(f32[128,128]{1,0:T(8,128)S(1)} %get-tuple-element.40), channel_id=1, source_target_pairs={{0,16},{8,24},{16,0},{24,8},{32,48},{40,56},{48,32},{56,40},{64,80... | collective-permute-start | bytes 196616 | tf_op jit(solution)/shard_map/ppermute | solution.py:345
  58.4 5.8 %collective-permute-start.7 = (f32[128,128]{1,0:T(8,128)S(1)}, f32[128,128]{1,0:T(8,128)S(1)}, u32[]{:S(2)}, u32[]{:S(2)}) collective-permute-start(f32[128,128]{1,0:T(8,128)S(1)} %get-tuple-element.41), channel_id=1, source_target_pairs={{0,8},{8,16},{16,24},{24,0},{32,40},{40,48},{48,56},{56,32},{64,72... | collective-permute-start | bytes 196616 | tf_op jit(solution)/shard_map/ppermute | solution.py:345

commit v3 on v2

--- a/solution.py
+++ b/solution.py
@@ -12,10 +12,12 @@
 BLOCKS = 8
 HEADS = 4
 NY = 4
+EARLY = 2
 NZ = 8
 F32 = jnp.float32
 BF16 = jnp.bfloat16
-VMEM_LIMIT = 48 * 1024 * 1024
+VMEM_LIMIT = 53 * 1024 * 1024
+TERMS_LIMIT = 60 * 1024 * 1024
 OUTPUTS_LIMIT = 48 * 1024 * 1024
 SMALL_LIMIT = 16 * 1024 * 1024
 PER = 2
@@ -98,7 +100,21 @@
     return both(rows, 0)
 
 
-def local_maps_kernel(k_ref, v_ref, b_ref, wu_ref, r_ref, tot_ref):
+def local_maps_kernel(k_all, v_all, b_ref, wu_ref, r_ref, tot_ref, k_held, v_held, arrived):
+    step_now = pl.program_id(0)
+
+    def fetch(source, held, which, step):
+        columns = pl.ds(pl.multiple_of(step * PER * 2 * D, PER * 2 * D), PER * 2 * D)
+        return pltpu.make_async_copy(source.at[:, columns], held.at[step], arrived.at[which, step])
+
+    @pl.when(step_now == 0)
+    def _():
+        for step in range(HEADS // PER):
+            fetch(k_all, k_held, 0, step).start()
+            fetch(v_all, v_held, 1, step).start()
+
+    fetch(k_all, k_held, 0, step_now).wait()
+    k_ref, v_ref = k_held.at[step_now], v_held.at[step_now]
     shape = (ITEMS, ITEMS)
     ni, nj = order(shape, 0), order(shape, 1)
     eye = (ni == nj).astype(F32)
@@ -142,6 +158,7 @@
         else:
             inv = [t - x for t, x in zip(inv, step)]
     maps = []
+    fetch(v_all, v_held, 1, step_now).wait()
     for i, (h, b) in enumerate(units):
         v = block_keys(v_ref, h, b)
         w = mm(both(split(inv[i] * beta_rk2[i : i + 1]), 1), both([keys[i], keys[i]], 0))
@@ -172,8 +189,8 @@
         local_maps_kernel,
         grid=(HEADS // PER,),
         in_specs=[
-            pl.BlockSpec((BLOCKS * HALF, PER * 2 * D), lambda h: (0, h)),
-            pl.BlockSpec((BLOCKS * HALF, PER * 2 * D), lambda h: (0, h)),
+            pl.BlockSpec(memory_space=pltpu.HBM),
+            pl.BlockSpec(memory_space=pltpu.HBM),
             pl.BlockSpec((2 * HEADS, BLOCKS * HALF), lambda h: (0, 0)),
         ],
         out_specs=[
@@ -186,16 +203,31 @@
             jax.ShapeDtypeStruct((HEADS, BLOCKS - 1, D, 4 * D), BF16),
             jax.ShapeDtypeStruct((HEADS, D, 2 * D), F32),
         ],
+        scratch_shapes=[
+            pltpu.VMEM((HEADS // PER, BLOCKS * HALF, PER * 2 * D), BF16),
+            pltpu.VMEM((HEADS // PER, BLOCKS * HALF, PER * 2 * D), BF16),
+            pltpu.SemaphoreType.DMA((2, HEADS // PER)),
+        ],
         compiler_params=pltpu.CompilerParams(vmem_limit_bytes=VMEM_LIMIT),
         name="local_maps",
     )(keys, values, betas)
 
 
-def outputs_kernel(q_ref, k_ref, wu_ref, r_ref, qe_ref, ol_ref):
+def block_terms(q_ref, k_ref, wu_ref, b):
     shape = (HALF, ITEMS)
     seen = (
         lax.broadcasted_iota(jnp.int32, shape, 1) % HALF <= lax.broadcasted_iota(jnp.int32, shape, 0)
     ).astype(F32)
+    q = q_ref[b * HALF : (b + 1) * HALF, :]
+    qf = q.astype(F32)
+    sh, sl = split(mm_nt(q, block_keys(k_ref, 0, b)) * seen)
+    wu = wu_ref[0, b]
+    x = wide3(sh, sl, wu[:, : 2 * D], wu[:, 2 * D :])
+    rq = lax.rsqrt(jnp.sum(qf * qf, -1, keepdims=True) + 1e-06)
+    return (qf - x[:, :D]) * rq, x[:, D:] * rq
+
+
+def entry_terms(terms, r_ref, qe_ref, ol_ref):
     node = [None] + [(r_ref[0, b][:, : 2 * D], r_ref[0, b][:, 2 * D :]) for b in range(BLOCKS - 1)]
 
     def onto(early, late):
@@ -210,40 +242,52 @@
     prefix[7] = onto(prefix[6], node[7])
     for b in range(BLOCKS):
         rows = slice(b * HALF, (b + 1) * HALF)
-        q = q_ref[rows, :]
-        qf = q.astype(F32)
-        sh, sl = split(mm_nt(q, block_keys(k_ref, 0, b)) * seen)
-        wu = wu_ref[0, b]
-        x = wide3(sh, sl, wu[:, : 2 * D], wu[:, 2 * D :])
-        qe, ol = qf - x[:, :D], x[:, D:]
+        qe, ol = terms(b)
         if b:
-            e = wide3(*split(qe), *prefix[b])
-            qe, ol = e[:, :D], e[:, D:] + ol
-        rq = lax.rsqrt(jnp.sum(qf * qf, -1, keepdims=True) + 1e-06)
-        qe_ref[0, rows, :] = qe * rq
-        ol_ref[0, rows, :] = ol * rq
-
-
-def local_outputs(queries, keys, wu, prefixes):
-    flops = 2 * HEADS * BLOCKS * HALF * D * D * 16
+            x = wide3(*split(qe), *prefix[b])
+            qe, ol = x[:, :D], x[:, D:] + ol
+        qe_ref[0, rows, :] = qe
+        ol_ref[0, rows, :] = ol
+
+
+def first_terms_kernel(q_ref, k_ref, wu_ref, qe_ref, ol_ref):
+    for b in range(BLOCKS):
+        rows = slice(b * HALF, (b + 1) * HALF)
+        qe_ref[0, rows, :], ol_ref[0, rows, :] = block_terms(q_ref, k_ref, wu_ref, b)
+
+
+def first_outputs_kernel(qb_ref, ob_ref, r_ref, qe_ref, ol_ref):
+    def terms(b):
+        rows = slice(b * HALF, (b + 1) * HALF)
+        return qb_ref[0, rows, :], ob_ref[0, rows, :]
+
+    entry_terms(terms, r_ref, qe_ref, ol_ref)
+
+
+def last_outputs_kernel(q_ref, k_ref, wu_ref, r_ref, qe_ref, ol_ref):
+    entry_terms(functools.partial(block_terms, q_ref, k_ref, wu_ref), r_ref, qe_ref, ol_ref)
+
+
+def per_head(kernel, name, arrays, kinds, first, heads, units, limit):
+    makers = {
+        "q": pl.BlockSpec((BLOCKS * HALF, D), lambda h: (0, h + first)),
+        "k": pl.BlockSpec((BLOCKS * HALF, 2 * D), lambda h: (0, h + first)),
+        "w": pl.BlockSpec((1, BLOCKS, ITEMS, 4 * D), lambda h: (h + first, 0, 0, 0)),
+        "r": pl.BlockSpec((1, BLOCKS - 1, D, 4 * D), lambda h: (h + first, 0, 0, 0)),
+        "t": pl.BlockSpec((1, BLOCKS * HALF, D), lambda h: (h, 0, 0)),
+    }
     return pl.pallas_call(
-        outputs_kernel,
-        grid=(HEADS,),
-        in_specs=[
-            pl.BlockSpec((BLOCKS * HALF, D), lambda h: (0, h)),
-            pl.BlockSpec((BLOCKS * HALF, 2 * D), lambda h: (0, h)),
-            pl.BlockSpec((1, BLOCKS, ITEMS, 4 * D), lambda h: (h, 0, 0, 0)),
-            pl.BlockSpec((1, BLOCKS - 1, D, 4 * D), lambda h: (h, 0, 0, 0)),
-        ],
-        out_specs=[
-            pl.BlockSpec((1, BLOCKS * HALF, D), lambda h: (h, 0, 0)),
-            pl.BlockSpec((1, BLOCKS * HALF, D), lambda h: (h, 0, 0)),
-        ],
-        out_shape=[jax.ShapeDtypeStruct((HEADS, BLOCKS * HALF, D), F32)] * 2,
-        compiler_params=pltpu.CompilerParams(vmem_limit_bytes=OUTPUTS_LIMIT),
-        cost_estimate=pl.CostEstimate(flops=flops, bytes_accessed=12 * 1024 * 1024, transcendentals=0),
-        name="local_outputs",
-    )(queries, keys, wu, prefixes)
+        kernel,
+        grid=(heads,),
+        in_specs=[makers[kind] for kind in kinds],
+        out_specs=[makers["t"]] * 2,
+        out_shape=[jax.ShapeDtypeStruct((heads, BLOCKS * HALF, D), F32)] * 2,
+        compiler_params=pltpu.CompilerParams(vmem_limit_bytes=limit),
+        cost_estimate=pl.CostEstimate(
+            flops=2 * heads * BLOCKS * HALF * D * D * units, bytes_accessed=6 * 1024 * 1024, transcendentals=0
+        ),
+        name=name,
+    )(*arrays)
 
 
 def in_vmem(n):
@@ -298,14 +342,15 @@
         out_ref[i] = apply(rows_ref[i - 1], state)
 
 
-def finish_kernel(me_ref, s_own, s1, s2, s3, qe_ref, ol_ref, g_ref, out_ref):
+def finish_kernel(me_ref, s0, s1, s2, s3, qa_ref, oa_ref, qb_ref, ob_ref, g_ref, out_ref, held):
     y = me_ref[0]
-    for s in range(NY):
-        h = (y + NY - s) % NY
-        state = (s_own, s1, s2, s3)[s][...]
-        raw = narrow3(*split(qe_ref[h]), *split(state)) + ol_ref[h]
+    for s, ref in enumerate((s0, s1, s2, s3)):
+        held[(y + NY - s) % NY] = ref[...]
+    for h in range(HEADS):
+        qe, ol = (qa_ref[h], oa_ref[h]) if h < EARLY else (qb_ref[h - EARLY], ob_ref[h - EARLY])
+        raw = narrow3(*split(qe), *split(held[h])) + ol
         scale = lax.rsqrt(jnp.mean(raw * raw, -1, keepdims=True) + 1e-06)
-        out_ref[:, pl.ds(pl.multiple_of(h * D, D), D)] = (raw * scale * g_ref[h]).astype(BF16)
+        out_ref[:, h * D : (h + 1) * D] = (raw * scale * g_ref[h]).astype(BF16)
 
 
 def call(kernel, n_in, out_shape, scratch=(), name=None):
@@ -344,12 +389,29 @@
         mine = [lax.dynamic_index_in_dim(array, (y + s) % NY, 0, False) for s in range(NY)]
         return mine[:1] + [lax.ppermute(mine[s], "ctx", shift_y(s)) for s in (1, 2, 3)]
 
+    arrived = exchange(total)
+    terms = per_head(
+        first_terms_kernel, "first_terms", (queries, keys, wu), "qkw", 0, EARLY, 7, TERMS_LIMIT
+    )
+    arrived, terms = lax.optimization_barrier((arrived, terms))
     rows_pre, row_total = call(
         row_maps_kernel, 4, [f32(3, D, 2 * D), f32(D, 2 * D)], [pltpu.VMEM((4, D, 2 * D), F32)], "row_maps"
-    )(me, *exchange(total))
+    )(me, *arrived)
     others = [lax.ppermute(row_total, "ctx", shift_z(s)) for s in (1, 2, 3)]
-    qe, ol = local_outputs(queries, keys, wu, prefixes)
-    others, qe, ol = lax.optimization_barrier((others, qe, ol))
+    first = per_head(
+        first_outputs_kernel, "first_outputs", (*terms, prefixes), "ttr", 0, EARLY, 10, OUTPUTS_LIMIT
+    )
+    last = per_head(
+        last_outputs_kernel,
+        "last_outputs",
+        (queries, keys, wu, prefixes),
+        "qkwr",
+        EARLY,
+        HEADS - EARLY,
+        17,
+        OUTPUTS_LIMIT,
+    )
+    others, first, last = lax.optimization_barrier((others, first, last))
     plane_pre, end, start = call(
         plane_maps_kernel,
         5,
@@ -360,8 +422,12 @@
     mid = lax.ppermute(end, "ctx", ACROSS)
     states = call(states_kernel, 4, f32(NY, D, D), (), "states")(me, start, mid, plane_pre, rows_pre)
     local_out = call(
-        finish_kernel, 7, jax.ShapeDtypeStruct((BLOCKS * HALF, HEADS * D), BF16), (), "finish"
-    )(me, *exchange(states), qe, ol, out_gain.reshape(HEADS, 1, D))
+        finish_kernel,
+        9,
+        jax.ShapeDtypeStruct((BLOCKS * HALF, HEADS * D), BF16),
+        [pltpu.VMEM((NY, D, D), F32)],
+        "finish",
+    )(me, *exchange(states), *first, *last, out_gain.reshape(HEADS, 1, D))
     return lax.all_to_all(local_out, "head", split_axis=0, concat_axis=1, tiled=True)
 
 

time: 81.1 us -> 78.9 us (0.973)
  waiting for transfers between devices: 15.7 us -> 12 us
  local copies, waits for them, and re-layouts: 5.12 us -> 1.67 us
  Pallas kernels: 27.9 us -> 31 us
  starting transfers between devices: 17.3 us -> 19.3 us
    ppermute x6, waiting for transfers between devices: 12.6 us -> 8.33 us  [exchange(): lax.ppermute(mine[s], 'ctx', shift_y(s))]
    unnamed x14 -> x16, local copies, waits for them, and re-layouts: 4.22 us -> 0.75 us
    ppermute x1, starting transfers between devices: 4.23 us -> 6.22 us  [body(): mid = lax.ppermute(end, 'ctx', ACROSS)]
    pallas_call x2 -> x4, Pallas kernels: 10.5 us -> 12.4 us  [the longest x3 11.2 us: per_head(): pl.pallas_call(kernel, grid=(heads,), in_specs=[makers[kind] for kind in...]
    ppermute x3, waiting for transfers between devices: 0.01 us -> 1.43 us  [body(): others = [lax.ppermute(row_total, 'ctx', shift_z(s)) for s in (1, 2, 3)]]
    pallas_call x1, Pallas kernels: 14.1 us -> 15.3 us  [local_maps(): pl.pallas_call(local_maps_kernel, grid=(HEADS // PER,), in_specs=[pl.Bloc...]
    ppermute x1, waiting for transfers between devices: 3.13 us -> 2.25 us  [body(): mid = lax.ppermute(end, 'ctx', ACROSS)]
  transfers between devices with their start and end apart: 10 -> 10, of which waited for: 7 -> 7; matrix products, arithmetic and copies ran while one was open for 0% -> 0% of each run, Pallas kernels for 12% -> 14%
where the time goes in v3:
time: 78.9 us; the launch traced here: 78.7 us
  Pallas kernels  31 us (39%)
  starting transfers between devices  19.3 us (24%)
  blocking collectives  14.5 us (18%)
  waiting for transfers between devices  12 us (15%)
  local copies, waits for them, and re-layouts  1.67 us (2%)
    pallas_call x1, Pallas kernels, local_maps(): pl.pallas_call(local_maps_kernel, grid=(HEADS // PER,), in_specs=[pl.Bloc...  15.3 us
    all_to_all x1, blocking collectives, body(): lax.all_to_all(local_out, 'head', split_axis=0, concat_axis=1, tiled=True)  14.5 us
    pallas_call x3, Pallas kernels, per_head(): pl.pallas_call(kernel, grid=(heads,), in_specs=[makers[kind] for kind in...  11.2 us
    ppermute x6, waiting for transfers between devices, exchange(): lax.ppermute(mine[s], 'ctx', shift_y(s))  8.33 us
    ppermute x6, starting transfers between devices, exchange(): lax.ppermute(mine[s], 'ctx', shift_y(s))  6.79 us
    ppermute x3, starting transfers between devices, body(): others = [lax.ppermute(row_total, 'ctx', shift_z(s)) for s in (1, 2, 3)]  6.27 us
    ppermute x1, starting transfers between devices, body(): mid = lax.ppermute(end, 'ctx', ACROSS)  6.22 us
    ppermute x1, waiting for transfers between devices, body(): mid = lax.ppermute(end, 'ctx', ACROSS)  2.25 us
  transfers between devices with their start and end apart: 10, of which 7 were waited for; matrix products, arithmetic and copies ran while one was open for 0% of the time, Pallas kernels for 14%

profile of v3, /device:TPU:32, one launch (start us, length us, event | category | flops | bytes accessed | tf_op | source)
XLA Modules:
  0.0 78.7 jit_solution(10720437105742801482)
XLA Ops:
  0.0 0.0 copy-start.6
  0.0 0.7 copy-done.6
  0.7 15.3 %local_maps.1 = (bf16[4,8,128,512]{3,2,1,0:T(8,128)(2,1)}, bf16[4,7,128,512]{3,2,1,0:T(8,128)(2,1)}, f32[4,128,256]{2,1,0:T(8,128)S(1)}) custom-call(bf16[512,1024]{1,0:T(8,128)(2,1)} %k_ref.3, bf16[512,1024]{1,0:T(8,128)(2,1)} %v_all.1, f32[8,512]{1,0:T(8,128)S(1)} %bitcast.25), custom_call_target="tpu_custom_call" | custom-call | tf_op jit(solution)/shard_map/local_maps/pallas_call | solution.py:188
  16.0 0.0 copy-start.1
  16.0 0.0 copy-start.2
  16.1 3.1 %collective-permute-start.2 = (f32[128,256]{1,0:T(8,128)S(1)}, f32[128,256]{1,0:T(8,128)S(1)}, u32[]{:S(2)}, u32[]{:S(2)}) collective-permute-start(f32[128,256]{1,0:T(8,128)S(1)} %get-tuple-element.59), channel_id=1, source_target_pairs={{0,24},{8,0},{16,8},{24,16},{32,56},{40,32},{48,40},{56,48},{64,88... | collective-permute-start | bytes 393224 | tf_op jit(solution)/shard_map/ppermute | solution.py:390
  19.2 0.6 collective-permute-start.1
  19.8 1.0 %collective-permute-start = (f32[128,256]{1,0:T(8,128)S(1)}, f32[128,256]{1,0:T(8,128)S(1)}, u32[]{:S(2)}, u32[]{:S(2)}) collective-permute-start(f32[128,256]{1,0:T(8,128)S(1)} %get-tuple-element.61), channel_id=1, source_target_pairs={{0,8},{8,16},{16,24},{24,0},{32,40},{40,48},{48,56},{56,32},{64,72... | collective-permute-start | bytes 393224 | tf_op jit(solution)/shard_map/ppermute | solution.py:390
  20.8 4.3 %first_terms.1 = (f32[2,512,128]{2,1,0:T(8,128)}, f32[2,512,128]{2,1,0:T(8,128)}) custom-call(bf16[512,512]{1,0:T(8,128)(2,1)} %q_ref.3, bf16[512,1024]{1,0:T(8,128)(2,1)} %k_ref.3, bf16[4,8,128,512]{3,2,1,0:T(8,128)(2,1)} %get-tuple-element.33.wu_ref), custom_call_target="tpu_custom_call" | custom-call | flops 234881024 | bytes 6291456 | tf_op jit(solution)/shard_map/first_terms/pallas_call | solution.py:279
  25.1 0.1 pad_add_fusion.me_ref
  25.2 0.0 collective-permute-done.2.r3
  25.2 1.8 %collective-permute-done.1.r2 = f32[128,256]{1,0:T(8,128)S(1)} collective-permute-done((f32[128,256]{1,0:T(8,128)S(1)}, f32[128,256]{1,0:T(8,128)S(1)}, u32[]{:S(2)}, u32[]{:S(2)}) %collective-permute-start.1) | collective-permute-done | bytes 131104 | tf_op jit(solution)/shard_map/ppermute | solution.py:390
  27.0 1.4 %collective-permute-done.r1 = f32[128,256]{1,0:T(8,128)S(1)} collective-permute-done((f32[128,256]{1,0:T(8,128)S(1)}, f32[128,256]{1,0:T(8,128)S(1)}, u32[]{:S(2)}, u32[]{:S(2)}) %collective-permute-start) | collective-permute-done | bytes 131104 | tf_op jit(solution)/shard_map/ppermute | solution.py:390
  28.4 1.0 %row_maps.1 = (f32[3,128,256]{2,1,0:T(8,128)S(1)}, f32[128,256]{1,0:T(8,128)S(1)}) custom-call(s32[2]{0:T(128)S(1)} %pad_add_fusion.me_ref, f32[128,256]{1,0:T(8,128)S(1)} %get-tuple-element.36.own_ref, f32[128,256]{1,0:T(8,128)S(1)} %collective-permute-done.r1, f32[128,256]{1,0:T(8,128)S(1)} %collective-permute-done.1.r2, ...), custom_call_target="tpu_custom_call" | custom-call | tf_op jit(solution)/shard_map/row_maps/pallas_call | solution.py:397
  29.5 0.2 collective-permute-start.5
  29.7 3.3 %collective-permute-start.4 = (f32[128,256]{1,0:T(8,128)S(1)}, f32[128,256]{1,0:T(8,128)S(1)}, u32[]{:S(2)}, u32[]{:S(2)}) collective-permute-start(f32[128,256]{1,0:T(8,128)S(1)} %get-tuple-element.40.own_ref), channel_id=1, source_target_pairs={{0,64},{8,72},{16,80},{24,88},{32,96},{40,104},{48,112},{56,120},{... | collective-permute-start | bytes 393224 | tf_op jit(solution)/shard_map/ppermute | solution.py:400
  32.9 2.8 %collective-permute-start.3 = (f32[128,256]{1,0:T(8,128)S(1)}, f32[128,256]{1,0:T(8,128)S(1)}, u32[]{:S(2)}, u32[]{:S(2)}) collective-permute-start(f32[128,256]{1,0:T(8,128)S(1)} %get-tuple-element.40.own_ref), channel_id=1, source_target_pairs={{0,32},{8,40},{16,48},{24,56},{32,64},{40,72},{48,80},{56,88},{64,... | collective-permute-start | bytes 393224 | tf_op jit(solution)/shard_map/ppermute | solution.py:400
  35.8 0.0 copy-done.1
  35.8 0.0 copy-done.2
  35.8 0.0 copy-start
  35.8 0.0 copy-start.3
  35.8 0.0 copy-start.4
  35.8 5.5 %last_outputs.1 = (f32[2,512,128]{2,1,0:T(8,128)S(1)}, f32[2,512,128]{2,1,0:T(8,128)S(1)}) custom-call(bf16[512,512]{1,0:T(8,128)(2,1)S(1)} %copy-done.2, bf16[512,1024]{1,0:T(8,128)(2,1)S(1)} %copy-done.1, bf16[4,8,128,512]{3,2,1,0:T(8,128)(2,1)} %get-tuple-element.33.wu_ref, bf16[4,7,128,512]{3,2,1,0:T(8,128)(2,1)} %get-tuple-element.43.r_ref), custom_call_target="tpu_custom_call" | custom-call | flops 570425344 | bytes 6291456 | tf_op jit(solution)/shard_map/last_outputs/pallas_call | solution.py:279
  41.3 0.0 copy-done
  41.3 0.0 copy-done.3
  41.4 0.0 copy-done.4
  41.4 0.0 copy-start.5
  41.4 0.0 copy-start.7
  41.4 1.4 %first_outputs.1 = (f32[2,512,128]{2,1,0:T(8,128)S(1)}, f32[2,512,128]{2,1,0:T(8,128)S(1)}) custom-call(f32[2,512,128]{2,1,0:T(8,128)S(1)} %copy-done.3, f32[2,512,128]{2,1,0:T(8,128)S(1)} %copy-done.4, bf16[4,7,128,512]{3,2,1,0:T(8,128)(2,1)S(1)} %copy-done), custom_call_target="tpu_custom_call" | custom-call | flops 335544320 | bytes 6291456 | tf_op jit(solution)/shard_map/first_outputs/pallas_call | solution.py:279
  42.8 0.0 collective-permute-done.5.r3
  42.8 0.0 collective-permute-done.4.r2
  42.8 1.4 %collective-permute-done.3.r1 = f32[128,256]{1,0:T(8,128)S(1)} collective-permute-done((f32[128,256]{1,0:T(8,128)S(1)}, f32[128,256]{1,0:T(8,128)S(1)}, u32[]{:S(2)}, u32[]{:S(2)}) %collective-permute-start.3) | collective-permute-done | bytes 131104 | tf_op jit(solution)/shard_map/ppermute | solution.py:400
  44.2 0.0 copy-done.5
  44.2 1.3 %plane_maps.1 = (f32[128,256]{1,0:T(8,128)S(1)}, f32[128,128]{1,0:T(8,128)S(1)}, f32[128,128]{1,0:T(8,128)S(1)}) custom-call(s32[2]{0:T(128)S(1)} %pad_add_fusion.me_ref, f32[128,256]{1,0:T(8,128)S(1)} %get-tuple-element.40.own_ref, f32[128,256]{1,0:T(8,128)S(1)} %collective-permute-done.3.r1, f32[128,256]{1,0:T(8,128)S(1)} %collective-permute-done.4.r2, ...), custom_call_target="tpu_custom_call" | custom-call | tf_op jit(solution)/shard_map/plane_maps/pallas_call | solution.py:415
  45.5 6.2 %collective-permute-start.6 = (f32[128,128]{1,0:T(8,128)S(1)}, f32[128,128]{1,0:T(8,128)S(1)}, u32[]{:S(2)}, u32[]{:S(2)}) collective-permute-start(f32[128,128]{1,0:T(8,128)S(1)} %get-tuple-element.52), channel_id=1, source_target_pairs={{0,224},{8,232},{16,240},{24,248},{32,192},{40,200},{48,208},{56,2... | collective-permute-start | bytes 196616 | tf_op jit(solution)/shard_map/ppermute | solution.py:422
  51.8 2.2 %collective-permute-done.6.mid_ref = f32[128,128]{1,0:T(8,128)S(1)} collective-permute-done((f32[128,128]{1,0:T(8,128)S(1)}, f32[128,128]{1,0:T(8,128)S(1)}, u32[]{:S(2)}, u32[]{:S(2)}) %collective-permute-start.6) | collective-permute-done | bytes 65568 | tf_op jit(solution)/shard_map/ppermute | solution.py:422
  54.0 0.9 %states.1 = f32[4,128,128]{2,1,0:T(8,128)S(1)} custom-call(s32[2]{0:T(128)S(1)} %pad_add_fusion.me_ref, f32[128,128]{1,0:T(8,128)S(1)} %get-tuple-element.51.s0t_ref, f32[128,128]{1,0:T(8,128)S(1)} %collective-permute-done.6.mid_ref, f32[128,256]{1,0:T(8,128)S(1)} %get-tuple-element.53.pre_ref, f32[3,128,256]{2,1,0:T(8,128)S(1)} %get-tuple-element.54.rows_ref), custom_call_target="tpu_custom_call" | custom-call | tf_op jit(solution)/shard_map/states/pallas_call | solution.py:423
  55.0 0.1 collective-permute-start.9
  55.1 0.1 collective-permute-start.8
  55.2 1.9 %collective-permute-start.7 = (f32[128,128]{1,0:T(8,128)S(1)}, f32[128,128]{1,0:T(8,128)S(1)}, u32[]{:S(2)}, u32[]{:S(2)}) collective-permute-start(f32[128,128]{1,0:T(8,128)S(1)} %get-tuple-element.65), channel_id=1, source_target_pairs={{0,8},{8,16},{16,24},{24,0},{32,40},{40,48},{48,56},{56,32},{64,72... | collective-permute-start | bytes 196616 | tf_op jit(solution)/shard_map/ppermute | solution.py:390
  57.1 2.2 %collective-permute-done.9.s3 = f32[128,128]{1,0:T(8,128)S(1)} collective-permute-done((f32[128,128]{1,0:T(8,128)S(1)}, f32[128,128]{1,0:T(8,128)S(1)}, u32[]{:S(2)}, u32[]{:S(2)}) %collective-permute-start.9) | collective-permute-done | bytes 65568 | tf_op jit(solution)/shard_map/ppermute | solution.py:390
  59.4 2.4 %collective-permute-done.8.s2 = f32[128,128]{1,0:T(8,128)S(1)} collective-permute-done((f32[128,128]{1,0:T(8,128)S(1)}, f32[128,128]{1,0:T(8,128)S(1)}, u32[]{:S(2)}, u32[]{:S(2)}) %collective-permute-start.8) | collective-permute-done | bytes 65568 | tf_op jit(solution)/shard_map/ppermute | solution.py:390
  61.7 0.5 collective-permute-done.7.s1
  62.2 0.0 copy-done.7
  62.2 1.1 %finish.1 = bf16[512,512]{1,0:T(8,128)(2,1)S(1)} custom-call(s32[2]{0:T(128)S(1)} %pad_add_fusion.me_ref, f32[128,128]{1,0:T(8,128)S(1)} %get-tuple-element.66.s0, f32[128,128]{1,0:T(8,128)S(1)} %collective-permute-done.7.s1, f32[128,128]{1,0:T(8,128)S(1)} %collective-permute-done.8.s2, f32[128,128]{1,0:T(8,128)S(1)} %collective-permute-done.9.s3, ...), custom_call_target="tpu_custom_call" | custom-call | tf_op jit(solution)/shard_map/finish/pallas_call | solution.py:424
  63.3 14.5 %all_to_all.19 = bf16[8,64,512]{2,1,0:T(8,128)(2,1)S(1)} all-to-all(bf16[8,64,512]{2,1,0:T(8,128)(2,1)S(1)} %bitcast.24), channel_id=1, replica_groups=mesh['ctx'=32,'head'=8] {'head'}, dimensions={0} | all-to-all | bytes 1048576 | tf_op jit(solution)/shard_map/all_to_all | solution.py:431
  77.8 0.8 %copy.8 = bf16[8,8,8,512]{3,2,0,1:T(8,128)(2,1)} copy(bf16[8,8,8,512]{3,2,1,0:T(8,128)(2,1)S(1)} %bitcast.27) | data formatting | bytes 1048576 | tf_op jit(solution)/shard_map/all_to_all | solution.py:431
  (2 shorter events, 0.1 us)
Async XLA Ops:
  0.0 0.7 copy-start.6
  16.0 19.8 %copy-start.1 = (bf16[512,1024]{1,0:T(8,128)(2,1)S(1)}, bf16[512,1024]{1,0:T(8,128)(2,1)}, u32[]{:S(2)}) copy-start(bf16[512,1024]{1,0:T(8,128)(2,1)} %k_ref.3) | copy-start | bytes 3145732
  16.0 19.8 %copy-start.2 = (bf16[512,512]{1,0:T(8,128)(2,1)S(1)}, bf16[512,512]{1,0:T(8,128)(2,1)}, u32[]{:S(2)}) copy-start(bf16[512,512]{1,0:T(8,128)(2,1)} %q_ref.3) | copy-start | bytes 1572868
  16.1 9.1 %collective-permute-start.2 = (f32[128,256]{1,0:T(8,128)S(1)}, f32[128,256]{1,0:T(8,128)S(1)}, u32[]{:S(2)}, u32[]{:S(2)}) collective-permute-start(f32[128,256]{1,0:T(8,128)S(1)} %get-tuple-element.59), channel_id=1, source_target_pairs={{0,24},{8,0},{16,8},{24,16},{32,56},{40,32},{48,40},{56,48},{64,88... | collective-permute-start | bytes 393224 | tf_op jit(solution)/shard_map/ppermute | solution.py:390
  19.2 7.9 %collective-permute-start.1 = (f32[128,256]{1,0:T(8,128)S(1)}, f32[128,256]{1,0:T(8,128)S(1)}, u32[]{:S(2)}, u32[]{:S(2)}) collective-permute-start(f32[128,256]{1,0:T(8,128)S(1)} %get-tuple-element.60), channel_id=1, source_target_pairs={{0,16},{8,24},{16,0},{24,8},{32,48},{40,56},{48,32},{56,40},{64,80... | collective-permute-start | bytes 393224 | tf_op jit(solution)/shard_map/ppermute | solution.py:390
  19.8 8.6 %collective-permute-start = (f32[128,256]{1,0:T(8,128)S(1)}, f32[128,256]{1,0:T(8,128)S(1)}, u32[]{:S(2)}, u32[]{:S(2)}) collective-permute-start(f32[128,256]{1,0:T(8,128)S(1)} %get-tuple-element.61), channel_id=1, source_target_pairs={{0,8},{8,16},{16,24},{24,0},{32,40},{40,48},{48,56},{56,32},{64,72... | collective-permute-start | bytes 393224 | tf_op jit(solution)/shard_map/ppermute | solution.py:390
  29.5 13.3 %collective-permute-start.5 = (f32[128,256]{1,0:T(8,128)S(1)}, f32[128,256]{1,0:T(8,128)S(1)}, u32[]{:S(2)}, u32[]{:S(2)}) collective-permute-start(f32[128,256]{1,0:T(8,128)S(1)} %get-tuple-element.40.own_ref), channel_id=1, source_target_pairs={{0,96},{8,104},{16,112},{24,120},{32,0},{40,8},{48,16},{56,24},{64... | collective-permute-start | bytes 393224 | tf_op jit(solution)/shard_map/ppermute | solution.py:400
  29.7 13.1 %collective-permute-start.4 = (f32[128,256]{1,0:T(8,128)S(1)}, f32[128,256]{1,0:T(8,128)S(1)}, u32[]{:S(2)}, u32[]{:S(2)}) collective-permute-start(f32[128,256]{1,0:T(8,128)S(1)} %get-tuple-element.40.own_ref), channel_id=1, source_target_pairs={{0,64},{8,72},{16,80},{24,88},{32,96},{40,104},{48,112},{56,120},{... | collective-permute-start | bytes 393224 | tf_op jit(solution)/shard_map/ppermute | solution.py:400
  32.9 11.3 %collective-permute-start.3 = (f32[128,256]{1,0:T(8,128)S(1)}, f32[128,256]{1,0:T(8,128)S(1)}, u32[]{:S(2)}, u32[]{:S(2)}) collective-permute-start(f32[128,256]{1,0:T(8,128)S(1)} %get-tuple-element.40.own_ref), channel_id=1, source_target_pairs={{0,32},{8,40},{16,48},{24,56},{32,64},{40,72},{48,80},{56,88},{64,... | collective-permute-start | bytes 393224 | tf_op jit(solution)/shard_map/ppermute | solution.py:400
  35.8 5.6 %copy-start = (bf16[4,7,128,512]{3,2,1,0:T(8,128)(2,1)S(1)}, bf16[4,7,128,512]{3,2,1,0:T(8,128)(2,1)}, u32[]{:S(2)}) copy-start(bf16[4,7,128,512]{3,2,1,0:T(8,128)(2,1)} %get-tuple-element.43.r_ref) | copy-start | bytes 11010052
  35.8 5.6 %copy-start.3 = (f32[2,512,128]{2,1,0:T(8,128)S(1)}, f32[2,512,128]{2,1,0:T(8,128)}, u32[]{:S(2)}) copy-start(f32[2,512,128]{2,1,0:T(8,128)} %get-tuple-element.41.qb_ref) | copy-start | bytes 1572868
  35.8 5.6 %copy-start.4 = (f32[2,512,128]{2,1,0:T(8,128)S(1)}, f32[2,512,128]{2,1,0:T(8,128)}, u32[]{:S(2)}) copy-start(f32[2,512,128]{2,1,0:T(8,128)} %get-tuple-element.42.ob_ref) | copy-start | bytes 1572868
  41.4 2.8 %copy-start.5 = (f32[4,128,128]{2,1,0:T(8,128)S(1)}, f32[4,128,128]{2,1,0:T(8,128)}, u32[]{:S(2)}) copy-start(f32[4,128,128]{2,1,0:T(8,128)} %s0_ref.1) | copy-start | bytes 786436
  41.4 20.8 %copy-start.7 = (f32[512]{0:T(512)S(1)}, f32[512]{0:T(512)}, u32[]{:S(2)}) copy-start(f32[512]{0:T(512)} %param.11) | copy-start | bytes 6148
  45.5 8.5 %collective-permute-start.6 = (f32[128,128]{1,0:T(8,128)S(1)}, f32[128,128]{1,0:T(8,128)S(1)}, u32[]{:S(2)}, u32[]{:S(2)}) collective-permute-start(f32[128,128]{1,0:T(8,128)S(1)} %get-tuple-element.52), channel_id=1, source_target_pairs={{0,224},{8,232},{16,240},{24,248},{32,192},{40,200},{48,208},{56,2... | collective-permute-start | bytes 196616 | tf_op jit(solution)/shard_map/ppermute | solution.py:422
  55.0 4.3 %collective-permute-start.9 = (f32[128,128]{1,0:T(8,128)S(1)}, f32[128,128]{1,0:T(8,128)S(1)}, u32[]{:S(2)}, u32[]{:S(2)}) collective-permute-start(f32[128,128]{1,0:T(8,128)S(1)} %get-tuple-element.63), channel_id=1, source_target_pairs={{0,24},{8,0},{16,8},{24,16},{32,56},{40,32},{48,40},{56,48},{64,88... | collective-permute-start | bytes 196616 | tf_op jit(solution)/shard_map/ppermute | solution.py:390
  55.1 6.6 %collective-permute-start.8 = (f32[128,128]{1,0:T(8,128)S(1)}, f32[128,128]{1,0:T(8,128)S(1)}, u32[]{:S(2)}, u32[]{:S(2)}) collective-permute-start(f32[128,128]{1,0:T(8,128)S(1)} %get-tuple-element.64), channel_id=1, source_target_pairs={{0,16},{8,24},{16,0},{24,8},{32,48},{40,56},{48,32},{56,40},{64,80... | collective-permute-start | bytes 196616 | tf_op jit(solution)/shard_map/ppermute | solution.py:390
  55.2 7.0 %collective-permute-start.7 = (f32[128,128]{1,0:T(8,128)S(1)}, f32[128,128]{1,0:T(8,128)S(1)}, u32[]{:S(2)}, u32[]{:S(2)}) collective-permute-start(f32[128,128]{1,0:T(8,128)S(1)} %get-tuple-element.65), channel_id=1, source_target_pairs={{0,8},{8,16},{16,24},{24,0},{32,40},{40,48},{48,56},{56,32},{64,72... | collective-permute-start | bytes 196616 | tf_op jit(solution)/shard_map/ppermute | solution.py:390

commit v4 on v3

--- a/solution.py
+++ b/solution.py
@@ -333,13 +333,21 @@
     return narrow3(*split(m[:, :D]), *split(state)) + m[:, D:]
 
 
-def states_kernel(me_ref, s0t_ref, mid_ref, pre_ref, rows_ref, out_ref):
-    z = me_ref[1]
-    base = jnp.where(z >= 4, mid_ref[...], s0t_ref[...])
-    state = jnp.where(z % 4 > 0, apply(pre_ref[...], base), base)
-    out_ref[0] = state
+def state_maps_kernel(me_ref, pre_ref, rows_ref, maps_ref):
+    inner = me_ref[1] % 4 > 0
+    pre = pre_ref[...]
+    i = lax.broadcasted_iota(jnp.int32, (D, 2 * D), 0)
+    j = lax.broadcasted_iota(jnp.int32, (D, 2 * D), 1)
+    maps_ref[0] = jnp.where(inner, pre, (i == j).astype(F32))
     for i in range(1, NY):
-        out_ref[i] = apply(rows_ref[i - 1], state)
+        late = rows_ref[i - 1]
+        maps_ref[i] = jnp.where(inner, join(pre, late), late)
+
+
+def states_kernel(me_ref, s0t_ref, mid_ref, maps_ref, out_ref):
+    base = jnp.where(me_ref[1] >= 4, mid_ref[...], s0t_ref[...])
+    for i in range(NY):
+        out_ref[i] = apply(maps_ref[i], base)
 
 
 def finish_kernel(me_ref, s0, s1, s2, s3, qa_ref, oa_ref, qb_ref, ob_ref, g_ref, out_ref, held):
@@ -420,7 +428,9 @@
         "plane_maps",
     )(me, row_total, *others, initial_state)
     mid = lax.ppermute(end, "ctx", ACROSS)
-    states = call(states_kernel, 4, f32(NY, D, D), (), "states")(me, start, mid, plane_pre, rows_pre)
+    maps = call(state_maps_kernel, 2, f32(NY, D, 2 * D), (), "state_maps")(me, plane_pre, rows_pre)
+    mid, maps = lax.optimization_barrier((mid, maps))
+    states = call(states_kernel, 3, f32(NY, D, D), (), "states")(me, start, mid, maps)
     local_out = call(
         finish_kernel,
         9,

time: 78.9 us -> 78.7 us (level)
  waiting for transfers between devices: 12 us -> 11.2 us
    ppermute x1, waiting for transfers between devices: 2.25 us -> 1.43 us  [body(): mid = lax.ppermute(end, 'ctx', ACROSS)]
    pallas_call x1 -> x2, Pallas kernels: 0.95 us -> 1.59 us  [the longest x1 0.81 us: body(): call(state_maps_kernel, 2, f32(NY, D, 2 * D), (), 'state_maps')]
  transfers between devices with their start and end apart: 10 -> 10, of which waited for: 7 -> 7; matrix products, arithmetic and copies ran while one was open for 0% -> 0% of each run, Pallas kernels for 14% -> 15%
where the time goes in v4:
time: 78.7 us; the launch traced here: 78.5 us
  Pallas kernels  31.6 us (40%)
  starting transfers between devices  19.3 us (25%)
  blocking collectives  14.5 us (18%)
  waiting for transfers between devices  11.2 us (14%)
  local copies, waits for them, and re-layouts  1.67 us (2%)
    pallas_call x1, Pallas kernels, local_maps(): pl.pallas_call(local_maps_kernel, grid=(HEADS // PER,), in_specs=[pl.Bloc...  15.3 us
    all_to_all x1, blocking collectives, body(): lax.all_to_all(local_out, 'head', split_axis=0, concat_axis=1, tiled=True)  14.5 us
    pallas_call x3, Pallas kernels, per_head(): pl.pallas_call(kernel, grid=(heads,), in_specs=[makers[kind] for kind in...  11.2 us
    ppermute x6, waiting for transfers between devices, exchange(): lax.ppermute(mine[s], 'ctx', shift_y(s))  8.33 us
    ppermute x6, starting transfers between devices, exchange(): lax.ppermute(mine[s], 'ctx', shift_y(s))  6.79 us
    ppermute x3, starting transfers between devices, body(): others = [lax.ppermute(row_total, 'ctx', shift_z(s)) for s in (1, 2, 3)]  6.27 us
    ppermute x1, starting transfers between devices, body(): mid = lax.ppermute(end, 'ctx', ACROSS)  6.22 us
  transfers between devices with their start and end apart: 10, of which 7 were waited for; matrix products, arithmetic and copies ran while one was open for 0% of the time, Pallas kernels for 15%

profile of v4, /device:TPU:32, one launch (start us, length us, event | category | flops | bytes accessed | tf_op | source)
XLA Modules:
  0.0 78.5 jit_solution(905724493334628991)
XLA Ops:
  0.0 0.0 copy-start.6
  0.0 0.7 copy-done.6
  0.7 15.3 %local_maps.1 = (bf16[4,8,128,512]{3,2,1,0:T(8,128)(2,1)}, bf16[4,7,128,512]{3,2,1,0:T(8,128)(2,1)}, f32[4,128,256]{2,1,0:T(8,128)S(1)}) custom-call(bf16[512,1024]{1,0:T(8,128)(2,1)} %k_ref.3, bf16[512,1024]{1,0:T(8,128)(2,1)} %v_all.1, f32[8,512]{1,0:T(8,128)S(1)} %bitcast.25), custom_call_target="tpu_custom_call" | custom-call | tf_op jit(solution)/shard_map/local_maps/pallas_call | solution.py:188
  16.0 0.0 copy-start.1
  16.0 0.0 copy-start.2
  16.1 3.1 %collective-permute-start.2 = (f32[128,256]{1,0:T(8,128)S(1)}, f32[128,256]{1,0:T(8,128)S(1)}, u32[]{:S(2)}, u32[]{:S(2)}) collective-permute-start(f32[128,256]{1,0:T(8,128)S(1)} %get-tuple-element.63), channel_id=1, source_target_pairs={{0,24},{8,0},{16,8},{24,16},{32,56},{40,32},{48,40},{56,48},{64,88... | collective-permute-start | bytes 393224 | tf_op jit(solution)/shard_map/ppermute | solution.py:398
  19.2 0.6 collective-permute-start.1
  19.8 1.0 %collective-permute-start = (f32[128,256]{1,0:T(8,128)S(1)}, f32[128,256]{1,0:T(8,128)S(1)}, u32[]{:S(2)}, u32[]{:S(2)}) collective-permute-start(f32[128,256]{1,0:T(8,128)S(1)} %get-tuple-element.65), channel_id=1, source_target_pairs={{0,8},{8,16},{16,24},{24,0},{32,40},{40,48},{48,56},{56,32},{64,72... | collective-permute-start | bytes 393224 | tf_op jit(solution)/shard_map/ppermute | solution.py:398
  20.8 4.3 %first_terms.1 = (f32[2,512,128]{2,1,0:T(8,128)}, f32[2,512,128]{2,1,0:T(8,128)}) custom-call(bf16[512,512]{1,0:T(8,128)(2,1)} %q_ref.3, bf16[512,1024]{1,0:T(8,128)(2,1)} %k_ref.3, bf16[4,8,128,512]{3,2,1,0:T(8,128)(2,1)} %get-tuple-element.35.wu_ref), custom_call_target="tpu_custom_call" | custom-call | flops 234881024 | bytes 6291456 | tf_op jit(solution)/shard_map/first_terms/pallas_call | solution.py:279
  25.1 0.1 pad_add_fusion.me_ref
  25.2 0.0 collective-permute-done.2.r3
  25.2 1.8 %collective-permute-done.1.r2 = f32[128,256]{1,0:T(8,128)S(1)} collective-permute-done((f32[128,256]{1,0:T(8,128)S(1)}, f32[128,256]{1,0:T(8,128)S(1)}, u32[]{:S(2)}, u32[]{:S(2)}) %collective-permute-start.1) | collective-permute-done | bytes 131104 | tf_op jit(solution)/shard_map/ppermute | solution.py:398
  27.0 1.4 %collective-permute-done.r1 = f32[128,256]{1,0:T(8,128)S(1)} collective-permute-done((f32[128,256]{1,0:T(8,128)S(1)}, f32[128,256]{1,0:T(8,128)S(1)}, u32[]{:S(2)}, u32[]{:S(2)}) %collective-permute-start) | collective-permute-done | bytes 131104 | tf_op jit(solution)/shard_map/ppermute | solution.py:398
  28.4 1.0 %row_maps.1 = (f32[3,128,256]{2,1,0:T(8,128)S(1)}, f32[128,256]{1,0:T(8,128)S(1)}) custom-call(s32[2]{0:T(128)S(1)} %pad_add_fusion.me_ref, f32[128,256]{1,0:T(8,128)S(1)} %get-tuple-element.38.own_ref, f32[128,256]{1,0:T(8,128)S(1)} %collective-permute-done.r1, f32[128,256]{1,0:T(8,128)S(1)} %collective-permute-done.1.r2, ...), custom_call_target="tpu_custom_call" | custom-call | tf_op jit(solution)/shard_map/row_maps/pallas_call | solution.py:405
  29.5 0.2 collective-permute-start.5
  29.7 3.3 %collective-permute-start.4 = (f32[128,256]{1,0:T(8,128)S(1)}, f32[128,256]{1,0:T(8,128)S(1)}, u32[]{:S(2)}, u32[]{:S(2)}) collective-permute-start(f32[128,256]{1,0:T(8,128)S(1)} %get-tuple-element.42.own_ref), channel_id=1, source_target_pairs={{0,64},{8,72},{16,80},{24,88},{32,96},{40,104},{48,112},{56,120},{... | collective-permute-start | bytes 393224 | tf_op jit(solution)/shard_map/ppermute | solution.py:408
  32.9 2.8 %collective-permute-start.3 = (f32[128,256]{1,0:T(8,128)S(1)}, f32[128,256]{1,0:T(8,128)S(1)}, u32[]{:S(2)}, u32[]{:S(2)}) collective-permute-start(f32[128,256]{1,0:T(8,128)S(1)} %get-tuple-element.42.own_ref), channel_id=1, source_target_pairs={{0,32},{8,40},{16,48},{24,56},{32,64},{40,72},{48,80},{56,88},{64,... | collective-permute-start | bytes 393224 | tf_op jit(solution)/shard_map/ppermute | solution.py:408
  35.8 0.0 copy-done.1
  35.8 0.0 copy-done.2
  35.8 0.0 copy-start
  35.8 0.0 copy-start.3
  35.8 0.0 copy-start.4
  35.8 5.5 %last_outputs.1 = (f32[2,512,128]{2,1,0:T(8,128)S(1)}, f32[2,512,128]{2,1,0:T(8,128)S(1)}) custom-call(bf16[512,512]{1,0:T(8,128)(2,1)S(1)} %copy-done.2, bf16[512,1024]{1,0:T(8,128)(2,1)S(1)} %copy-done.1, bf16[4,8,128,512]{3,2,1,0:T(8,128)(2,1)} %get-tuple-element.35.wu_ref, bf16[4,7,128,512]{3,2,1,0:T(8,128)(2,1)} %get-tuple-element.45.r_ref), custom_call_target="tpu_custom_call" | custom-call | flops 570425344 | bytes 6291456 | tf_op jit(solution)/shard_map/last_outputs/pallas_call | solution.py:279
  41.3 0.0 copy-done
  41.3 0.0 copy-done.3
  41.4 0.0 copy-done.4
  41.4 0.0 copy-start.5
  41.4 0.0 copy-start.7
  41.4 1.4 %first_outputs.1 = (f32[2,512,128]{2,1,0:T(8,128)S(1)}, f32[2,512,128]{2,1,0:T(8,128)S(1)}) custom-call(f32[2,512,128]{2,1,0:T(8,128)S(1)} %copy-done.3, f32[2,512,128]{2,1,0:T(8,128)S(1)} %copy-done.4, bf16[4,7,128,512]{3,2,1,0:T(8,128)(2,1)S(1)} %copy-done), custom_call_target="tpu_custom_call" | custom-call | flops 335544320 | bytes 6291456 | tf_op jit(solution)/shard_map/first_outputs/pallas_call | solution.py:279
  42.8 0.0 collective-permute-done.5.r3
  42.8 0.0 collective-permute-done.4.r2
  42.8 1.4 %collective-permute-done.3.r1 = f32[128,256]{1,0:T(8,128)S(1)} collective-permute-done((f32[128,256]{1,0:T(8,128)S(1)}, f32[128,256]{1,0:T(8,128)S(1)}, u32[]{:S(2)}, u32[]{:S(2)}) %collective-permute-start.3) | collective-permute-done | bytes 131104 | tf_op jit(solution)/shard_map/ppermute | solution.py:408
  44.2 0.0 copy-done.5
  44.2 1.3 %plane_maps.1 = (f32[128,256]{1,0:T(8,128)S(1)}, f32[128,128]{1,0:T(8,128)S(1)}, f32[128,128]{1,0:T(8,128)S(1)}) custom-call(s32[2]{0:T(128)S(1)} %pad_add_fusion.me_ref, f32[128,256]{1,0:T(8,128)S(1)} %get-tuple-element.42.own_ref, f32[128,256]{1,0:T(8,128)S(1)} %collective-permute-done.3.r1, f32[128,256]{1,0:T(8,128)S(1)} %collective-permute-done.4.r2, ...), custom_call_target="tpu_custom_call" | custom-call | tf_op jit(solution)/shard_map/plane_maps/pallas_call | solution.py:423
  45.5 6.2 %collective-permute-start.6 = (f32[128,128]{1,0:T(8,128)S(1)}, f32[128,128]{1,0:T(8,128)S(1)}, u32[]{:S(2)}, u32[]{:S(2)}) collective-permute-start(f32[128,128]{1,0:T(8,128)S(1)} %get-tuple-element.54), channel_id=1, source_target_pairs={{0,224},{8,232},{16,240},{24,248},{32,192},{40,200},{48,208},{56,2... | collective-permute-start | bytes 196616 | tf_op jit(solution)/shard_map/ppermute | solution.py:430
  51.8 0.8 %state_maps.1.maps_ref = f32[4,128,256]{2,1,0:T(8,128)S(1)} custom-call(s32[2]{0:T(128)S(1)} %pad_add_fusion.me_ref, f32[128,256]{1,0:T(8,128)S(1)} %get-tuple-element.55.pre_ref, f32[3,128,256]{2,1,0:T(8,128)S(1)} %get-tuple-element.56.rows_ref), custom_call_target="tpu_custom_call" | custom-call | tf_op jit(solution)/shard_map/state_maps/pallas_call | solution.py:431
  52.6 1.4 %collective-permute-done.6.mid_ref = f32[128,128]{1,0:T(8,128)S(1)} collective-permute-done((f32[128,128]{1,0:T(8,128)S(1)}, f32[128,128]{1,0:T(8,128)S(1)}, u32[]{:S(2)}, u32[]{:S(2)}) %collective-permute-start.6) | collective-permute-done | bytes 65568 | tf_op jit(solution)/shard_map/ppermute | solution.py:430
  54.0 0.8 states.1
  54.8 0.1 collective-permute-start.9
  54.9 0.1 collective-permute-start.8
  55.0 1.9 %collective-permute-start.7 = (f32[128,128]{1,0:T(8,128)S(1)}, f32[128,128]{1,0:T(8,128)S(1)}, u32[]{:S(2)}, u32[]{:S(2)}) collective-permute-start(f32[128,128]{1,0:T(8,128)S(1)} %get-tuple-element.69), channel_id=1, source_target_pairs={{0,8},{8,16},{16,24},{24,0},{32,40},{40,48},{48,56},{56,32},{64,72... | collective-permute-start | bytes 196616 | tf_op jit(solution)/shard_map/ppermute | solution.py:398
  56.9 2.2 %collective-permute-done.9.s3 = f32[128,128]{1,0:T(8,128)S(1)} collective-permute-done((f32[128,128]{1,0:T(8,128)S(1)}, f32[128,128]{1,0:T(8,128)S(1)}, u32[]{:S(2)}, u32[]{:S(2)}) %collective-permute-start.9) | collective-permute-done | bytes 65568 | tf_op jit(solution)/shard_map/ppermute | solution.py:398
  59.2 2.4 %collective-permute-done.8.s2 = f32[128,128]{1,0:T(8,128)S(1)} collective-permute-done((f32[128,128]{1,0:T(8,128)S(1)}, f32[128,128]{1,0:T(8,128)S(1)}, u32[]{:S(2)}, u32[]{:S(2)}) %collective-permute-start.8) | collective-permute-done | bytes 65568 | tf_op jit(solution)/shard_map/ppermute | solution.py:398
  61.6 0.5 collective-permute-done.7.s1
  62.0 0.0 copy-done.7
  62.0 1.1 %finish.1 = bf16[512,512]{1,0:T(8,128)(2,1)S(1)} custom-call(s32[2]{0:T(128)S(1)} %pad_add_fusion.me_ref, f32[128,128]{1,0:T(8,128)S(1)} %get-tuple-element.70.s0, f32[128,128]{1,0:T(8,128)S(1)} %collective-permute-done.7.s1, f32[128,128]{1,0:T(8,128)S(1)} %collective-permute-done.8.s2, f32[128,128]{1,0:T(8,128)S(1)} %collective-permute-done.9.s3, ...), custom_call_target="tpu_custom_call" | custom-call | tf_op jit(solution)/shard_map/finish/pallas_call | solution.py:434
  63.2 14.5 %all_to_all.19 = bf16[8,64,512]{2,1,0:T(8,128)(2,1)S(1)} all-to-all(bf16[8,64,512]{2,1,0:T(8,128)(2,1)S(1)} %bitcast.24), channel_id=1, replica_groups=mesh['ctx'=32,'head'=8] {'head'}, dimensions={0} | all-to-all | bytes 1048576 | tf_op jit(solution)/shard_map/all_to_all | solution.py:441
  77.7 0.8 %copy.8 = bf16[8,8,8,512]{3,2,0,1:T(8,128)(2,1)} copy(bf16[8,8,8,512]{3,2,1,0:T(8,128)(2,1)S(1)} %bitcast.27) | data formatting | bytes 1048576 | tf_op jit(solution)/shard_map/all_to_all | solution.py:441
  (2 shorter events, 0.1 us)
Async XLA Ops:
  0.0 0.7 copy-start.6
  16.0 19.8 %copy-start.1 = (bf16[512,1024]{1,0:T(8,128)(2,1)S(1)}, bf16[512,1024]{1,0:T(8,128)(2,1)}, u32[]{:S(2)}) copy-start(bf16[512,1024]{1,0:T(8,128)(2,1)} %k_ref.3) | copy-start | bytes 3145732
  16.0 19.8 %copy-start.2 = (bf16[512,512]{1,0:T(8,128)(2,1)S(1)}, bf16[512,512]{1,0:T(8,128)(2,1)}, u32[]{:S(2)}) copy-start(bf16[512,512]{1,0:T(8,128)(2,1)} %q_ref.3) | copy-start | bytes 1572868
  16.1 9.1 %collective-permute-start.2 = (f32[128,256]{1,0:T(8,128)S(1)}, f32[128,256]{1,0:T(8,128)S(1)}, u32[]{:S(2)}, u32[]{:S(2)}) collective-permute-start(f32[128,256]{1,0:T(8,128)S(1)} %get-tuple-element.63), channel_id=1, source_target_pairs={{0,24},{8,0},{16,8},{24,16},{32,56},{40,32},{48,40},{56,48},{64,88... | collective-permute-start | bytes 393224 | tf_op jit(solution)/shard_map/ppermute | solution.py:398
  19.2 7.9 %collective-permute-start.1 = (f32[128,256]{1,0:T(8,128)S(1)}, f32[128,256]{1,0:T(8,128)S(1)}, u32[]{:S(2)}, u32[]{:S(2)}) collective-permute-start(f32[128,256]{1,0:T(8,128)S(1)} %get-tuple-element.64), channel_id=1, source_target_pairs={{0,16},{8,24},{16,0},{24,8},{32,48},{40,56},{48,32},{56,40},{64,80... | collective-permute-start | bytes 393224 | tf_op jit(solution)/shard_map/ppermute | solution.py:398
  19.8 8.6 %collective-permute-start = (f32[128,256]{1,0:T(8,128)S(1)}, f32[128,256]{1,0:T(8,128)S(1)}, u32[]{:S(2)}, u32[]{:S(2)}) collective-permute-start(f32[128,256]{1,0:T(8,128)S(1)} %get-tuple-element.65), channel_id=1, source_target_pairs={{0,8},{8,16},{16,24},{24,0},{32,40},{40,48},{48,56},{56,32},{64,72... | collective-permute-start | bytes 393224 | tf_op jit(solution)/shard_map/ppermute | solution.py:398
  29.5 13.3 %collective-permute-start.5 = (f32[128,256]{1,0:T(8,128)S(1)}, f32[128,256]{1,0:T(8,128)S(1)}, u32[]{:S(2)}, u32[]{:S(2)}) collective-permute-start(f32[128,256]{1,0:T(8,128)S(1)} %get-tuple-element.42.own_ref), channel_id=1, source_target_pairs={{0,96},{8,104},{16,112},{24,120},{32,0},{40,8},{48,16},{56,24},{64... | collective-permute-start | bytes 393224 | tf_op jit(solution)/shard_map/ppermute | solution.py:408
  29.7 13.1 %collective-permute-start.4 = (f32[128,256]{1,0:T(8,128)S(1)}, f32[128,256]{1,0:T(8,128)S(1)}, u32[]{:S(2)}, u32[]{:S(2)}) collective-permute-start(f32[128,256]{1,0:T(8,128)S(1)} %get-tuple-element.42.own_ref), channel_id=1, source_target_pairs={{0,64},{8,72},{16,80},{24,88},{32,96},{40,104},{48,112},{56,120},{... | collective-permute-start | bytes 393224 | tf_op jit(solution)/shard_map/ppermute | solution.py:408
  32.9 11.3 %collective-permute-start.3 = (f32[128,256]{1,0:T(8,128)S(1)}, f32[128,256]{1,0:T(8,128)S(1)}, u32[]{:S(2)}, u32[]{:S(2)}) collective-permute-start(f32[128,256]{1,0:T(8,128)S(1)} %get-tuple-element.42.own_ref), channel_id=1, source_target_pairs={{0,32},{8,40},{16,48},{24,56},{32,64},{40,72},{48,80},{56,88},{64,... | collective-permute-start | bytes 393224 | tf_op jit(solution)/shard_map/ppermute | solution.py:408
  35.8 5.6 %copy-start = (bf16[4,7,128,512]{3,2,1,0:T(8,128)(2,1)S(1)}, bf16[4,7,128,512]{3,2,1,0:T(8,128)(2,1)}, u32[]{:S(2)}) copy-start(bf16[4,7,128,512]{3,2,1,0:T(8,128)(2,1)} %get-tuple-element.45.r_ref) | copy-start | bytes 11010052
  35.8 5.6 %copy-start.3 = (f32[2,512,128]{2,1,0:T(8,128)S(1)}, f32[2,512,128]{2,1,0:T(8,128)}, u32[]{:S(2)}) copy-start(f32[2,512,128]{2,1,0:T(8,128)} %get-tuple-element.43.qb_ref) | copy-start | bytes 1572868
  35.8 5.6 %copy-start.4 = (f32[2,512,128]{2,1,0:T(8,128)S(1)}, f32[2,512,128]{2,1,0:T(8,128)}, u32[]{:S(2)}) copy-start(f32[2,512,128]{2,1,0:T(8,128)} %get-tuple-element.44.ob_ref) | copy-start | bytes 1572868
  41.4 2.8 %copy-start.5 = (f32[4,128,128]{2,1,0:T(8,128)S(1)}, f32[4,128,128]{2,1,0:T(8,128)}, u32[]{:S(2)}) copy-start(f32[4,128,128]{2,1,0:T(8,128)} %s0_ref.1) | copy-start | bytes 786436
  41.4 20.6 %copy-start.7 = (f32[512]{0:T(512)S(1)}, f32[512]{0:T(512)}, u32[]{:S(2)}) copy-start(f32[512]{0:T(512)} %param.11) | copy-start | bytes 6148
  45.5 8.5 %collective-permute-start.6 = (f32[128,128]{1,0:T(8,128)S(1)}, f32[128,128]{1,0:T(8,128)S(1)}, u32[]{:S(2)}, u32[]{:S(2)}) collective-permute-start(f32[128,128]{1,0:T(8,128)S(1)} %get-tuple-element.54), channel_id=1, source_target_pairs={{0,224},{8,232},{16,240},{24,248},{32,192},{40,200},{48,208},{56,2... | collective-permute-start | bytes 196616 | tf_op jit(solution)/shard_map/ppermute | solution.py:430
  54.8 4.3 %collective-permute-start.9 = (f32[128,128]{1,0:T(8,128)S(1)}, f32[128,128]{1,0:T(8,128)S(1)}, u32[]{:S(2)}, u32[]{:S(2)}) collective-permute-start(f32[128,128]{1,0:T(8,128)S(1)} %get-tuple-element.67), channel_id=1, source_target_pairs={{0,24},{8,0},{16,8},{24,16},{32,56},{40,32},{48,40},{56,48},{64,88... | collective-permute-start | bytes 196616 | tf_op jit(solution)/shard_map/ppermute | solution.py:398
  54.9 6.6 %collective-permute-start.8 = (f32[128,128]{1,0:T(8,128)S(1)}, f32[128,128]{1,0:T(8,128)S(1)}, u32[]{:S(2)}, u32[]{:S(2)}) collective-permute-start(f32[128,128]{1,0:T(8,128)S(1)} %get-tuple-element.68), channel_id=1, source_target_pairs={{0,16},{8,24},{16,0},{24,8},{32,48},{40,56},{48,32},{56,40},{64,80... | collective-permute-start | bytes 196616 | tf_op jit(solution)/shard_map/ppermute | solution.py:398
  55.0 7.0 %collective-permute-start.7 = (f32[128,128]{1,0:T(8,128)S(1)}, f32[128,128]{1,0:T(8,128)S(1)}, u32[]{:S(2)}, u32[]{:S(2)}) collective-permute-start(f32[128,128]{1,0:T(8,128)S(1)} %get-tuple-element.69), channel_id=1, source_target_pairs={{0,8},{8,16},{16,24},{24,0},{32,40},{40,48},{48,56},{56,32},{64,72... | collective-permute-start | bytes 196616 | tf_op jit(solution)/shard_map/ppermute | solution.py:398
